TPU v7x, 32 devices: a whole 2x2x4 slice. The times are simulated.
32 devices in a mesh: section: 2 (over x), expert: 16 (over z, y, core).
Axes of the slice: x: 2, y: 2, z: 4, core: 2. Of those that a mesh axis runs over, the one named last changes fastest.
Arguments:
- next_grad: bfloat16 [2, 256, 3584], P('section', 'expert'), may hold values from -6 to 6
- routes: int32 [2, 256, 8], P('section', 'expert'), may hold values from 0 to 15, all different within a row; in each aligned block of 16 rows (0 to 15, 16 to 31, ..., all dimensions but the last counted through in order) at most 16 rows name the same one
- gates: float32 [2, 256, 8], P('section', 'expert'), may hold values from 0.1 to 0.6
- saved: bfloat16 [2, 16, 256, 2048], P('section', 'expert'), may hold values from -5 to 5
- w_down: bfloat16 [16, 1024, 3584], P('expert'), may hold values from -0.1875 to 0.1875
Outputs:
- hidden_grads: bfloat16 [2, 16, 256, 2048], P('section', 'expert')
Inputs may be any that keep to these rules, and one draw needn't show every extreme that they name: `routes`: each row names 8 different experts; among the 16 rows of one device no expert is named by more than 16 rows, and in every draw some expert is named by exactly 16 rows of some device.
All inputs are finite; a program needn't handle non-finite values.
Results may differ from a plain program's by a relative error of at most 0.005.
Values may be sent and summed in bfloat16 or wider, within the bound.
No kernel may reach another device: no remote copies, remote signals or barrier semaphores. Data moves between devices by JAX's collectives and lax.ppermute only.
A program may use at most 64 MiB of HBM per device.

v0:
```python
import jax
import jax.numpy as jnp
from jax import lax
from jax.sharding import PartitionSpec as P


def passed_along(x, axis, by):
    peers = lax.axis_size(axis)
    return lax.ppermute(x, axis, [(i, (i + by) % peers) for i in range(peers)])


def assign_table(routes, gates, experts):
    expert_ids = jnp.arange(experts, dtype=jnp.int32)
    match = routes[:, :, None] == expert_ids[None, None, :]
    return jnp.sum(jnp.where(match, gates[:, :, None], 0.0), axis=1)


def build_rows(grad, assign, most):
    live = (assign > 0.0).astype(jnp.int32)
    before = jnp.cumsum(live, axis=0) - live
    places = jnp.arange(most, dtype=jnp.int32)
    pick = (before[:, :, None] == places[None, None, :]) & (live[:, :, None] > 0)
    tok_rows = pick.shape[0]
    token_ids = jnp.arange(tok_rows, dtype=jnp.int32)[:, None, None]
    chosen = jnp.sum(jnp.where(pick, token_ids, 0), axis=0)
    weight = jnp.sum(jnp.where(pick, assign[:, :, None], 0.0), axis=0)
    filled = jnp.any(pick, axis=0)
    flat_ids = chosen.reshape(-1)
    taken = jnp.take(grad, flat_ids, axis=0).astype(jnp.float32)
    scaled = weight.reshape(-1)[:, None] * taken
    rows = jnp.where(filled.reshape(-1)[:, None], scaled, 0.0)
    return rows.astype(jnp.bfloat16).reshape(pick.shape[1], most, grad.shape[1])


def dispatch(rows):
    return lax.all_to_all(rows, "expert", split_axis=0, concat_axis=0, tiled=True)


def per_device(next_grad, routes, gates, saved, w_down):
    experts = lax.axis_size("expert")
    slots = saved.shape[2]
    most = slots // experts
    hidden_width = w_down.shape[1]
    assign = assign_table(routes[0], gates[0], experts)
    grad = passed_along(next_grad[0], "section", -1)
    received = dispatch(build_rows(grad, assign, most))
    received = received.reshape(slots, received.shape[2])
    hidden = lax.dot_general(
        received, w_down[0], (((1,), (1,)), ((), ())), preferred_element_type=jnp.float32
    )
    pre_gate = saved[0, 0, :, :hidden_width].astype(jnp.float32)
    pre_up = saved[0, 0, :, hidden_width:].astype(jnp.float32)
    sig = jax.nn.sigmoid(pre_gate)
    d_up = hidden * pre_gate * sig
    d_gate = hidden * pre_up * sig * (1.0 + pre_gate * (1.0 - sig))
    result = jnp.concatenate([d_gate, d_up], axis=-1).astype(jnp.bfloat16)
    return result[None, None]


def solution(mesh):
    return jax.shard_map(
        per_device,
        mesh=mesh,
        in_specs=(
            P("section", "expert", None),
            P("section", "expert", None),
            P("section", "expert", None),
            P("section", "expert", None, None),
            P("expert", None, None),
        ),
        out_specs=P("section", "expert", None, None),
        check_vma=False,
    )
```

profile of v0, /device:TPU:13, one launch (start us, length us, event | category | flops | bytes accessed | tf_op | source)
XLA Modules:
  0.0 64.2 jit_solution(16652889349469923936)
XLA Ops:
  0.0 1.2 %collective-permute-start = (bf16[16,3584]{1,0:T(8,128)(2,1)}, bf16[16,3584]{1,0:T(8,128)(2,1)S(1)}, u32[]{:S(2)}, u32[]{:S(2)}) collective-permute-start(bf16[16,3584]{1,0:T(8,128)(2,1)} %bitcast.34), channel_id=1, source_target_pairs={{0,16},{16,0},{1,17},{17,1},{2,18},{18,2},{3,19},{19,3},{4,20},{20... | collective-permute-start | bytes 344072 | tf_op jit(solution)/shard_map/ppermute | solution.py:9
  1.2 0.8 %copy.8 = s32[16,8]{1,0:T(8,128)S(1)} copy(s32[16,8]{0,1:T(8,128)} %bitcast.31) | data formatting | bytes 1024 | tf_op jit(solution)/shard_map/eq | solution.py:14
  2.0 0.8 %copy.9 = f32[16,8]{1,0:T(8,128)S(1)} copy(f32[16,8]{0,1:T(8,128)} %bitcast.32) | data formatting | bytes 1024 | tf_op jit(solution)/shard_map/jit(_where)/broadcast_in_dim | solution.py:15
  2.7 0.1 select_reduce_fusion.2
  2.9 0.2 select_reduce_fusion.1
  3.1 0.1 select_reduce_fusion
  3.2 0.1 reshape.114
  3.3 0.1 fusion.14
  3.5 0.8 %collective-permute-done = bf16[16,3584]{1,0:T(8,128)(2,1)S(1)} collective-permute-done((bf16[16,3584]{1,0:T(8,128)(2,1)}, bf16[16,3584]{1,0:T(8,128)(2,1)S(1)}, u32[]{:S(2)}, u32[]{:S(2)}) %collective-permute-start) | collective-permute-done | bytes 114720 | tf_op jit(solution)/shard_map/ppermute | solution.py:9
  4.2 1.7 %gather_fusion = bf16[256,3584]{1,0:T(8,128)(2,1)S(1)} fusion(bf16[16,3584]{1,0:T(8,128)(2,1)S(1)} %collective-permute-done, s32[1024]{0:T(1024)S(1)} %pad_clamp_fusion), kind=kCustom, calls=%fused_computation | custom fusion | bytes 3671040 | tf_op jit(solution)/shard_map/jit(_take)/gather | solution.py:29
  5.9 2.5 %select_convert_fusion = bf16[16,16,3584]{2,1,0:T(8,128)(2,1)} fusion(bf16[16,16,3584]{2,1,0:T(8,128)(2,1)S(1)} %bitcast.29, f32[16,16]{1,0:T(8,128)S(1)} %select_reduce_fusion.1, pred[16,16]{1,0:T(8,128)(4,1)S(1)} %compare_and_fusion, pred[16,16]{1,0:T(8,128)(4,1)S(1)} %fusion.14), kind=kLoop, calls=%fused_computation.3 | loop fusion | flops 4587520 | bytes 3671552 | tf_op jit(solution)/shard_map/convert_element_type | solution.py:32
  8.4 0.0 copy-start
  8.4 7.6 %all-to-all-start = ((bf16[16,16,3584]{2,1,0:T(8,128)(2,1)}), bf16[16,16,3584]{2,1,0:T(8,128)(2,1)S(1)}, u32[]{:S(2)}, u32[]{:S(2)}) async-start(bf16[16,16,3584]{2,1,0:T(8,128)(2,1)} %select_convert_fusion), calls=%async_computation | async-start | bytes 3670016 | tf_op jit(solution)/shard_map/all_to_all | solution.py:36
  16.0 41.8 %all-to-all-done = bf16[16,16,3584]{2,1,0:T(8,128)(2,1)S(1)} async-done(((bf16[16,16,3584]{2,1,0:T(8,128)(2,1)}), bf16[16,16,3584]{2,1,0:T(8,128)(2,1)S(1)}, u32[]{:S(2)}, u32[]{:S(2)}) %all-to-all-start) | async-done | bytes 1835040 | tf_op jit(solution)/shard_map/all_to_all | solution.py:36
  57.8 0.0 copy-done
  57.8 6.4 %fusion.12 = (bf16[1,1,256,2048]{3,2,1,0:T(8,128)(2,1)}, bf16[1,1,256,2048]{3,2,1,0:T(8,128)(2,1)}) fusion(bf16[1,1,256,2048]{3,2,1,0:T(8,128)(2,1)S(1)} %copy-done, bf16[256,3584]{1,0:T(8,128)(2,1)S(1)} %bitcast.30, bf16[1,1024,3584]{2,1,0:T(8,128)(2,1)} %param.9, ...), kind=kOutput, output_to_operand_aliasing={{0}: (3, {}), {1}: (3, {})}, calls=%fused_computation.19 | convolution fusion | flops 1882980352 | bytes 11272192 | tf_op jit(solution)/shard_map/dot_general | solution.py:48
  (7 shorter events, 0.1 us)
Async XLA Ops:
  0.0 4.2 %collective-permute-start = (bf16[16,3584]{1,0:T(8,128)(2,1)}, bf16[16,3584]{1,0:T(8,128)(2,1)S(1)}, u32[]{:S(2)}, u32[]{:S(2)}) collective-permute-start(bf16[16,3584]{1,0:T(8,128)(2,1)} %bitcast.34), channel_id=1, source_target_pairs={{0,16},{16,0},{1,17},{17,1},{2,18},{18,2},{3,19},{19,3},{4,20},{20... | collective-permute-start | bytes 344072 | tf_op jit(solution)/shard_map/ppermute | solution.py:9
  8.4 49.4 %copy-start = (bf16[1,1,256,2048]{3,2,1,0:T(8,128)(2,1)S(1)}, bf16[1,1,256,2048]{3,2,1,0:T(8,128)(2,1)}, u32[]{:S(2)}) copy-start(bf16[1,1,256,2048]{3,2,1,0:T(8,128)(2,1)} %param.8) | copy-start | bytes 3145732
  8.4 49.4 %all-to-all-start = ((bf16[16,16,3584]{2,1,0:T(8,128)(2,1)}), bf16[16,16,3584]{2,1,0:T(8,128)(2,1)S(1)}, u32[]{:S(2)}, u32[]{:S(2)}) async-start(bf16[16,16,3584]{2,1,0:T(8,128)(2,1)} %select_convert_fusion), calls=%async_computation | async-start | bytes 3670016 | tf_op jit(solution)/shard_map/all_to_all | solution.py:36
where the time goes:
time: 64.5 us; the launch traced here: 64.2 us
  waiting for transfers between devices  42.6 us (66%)
  starting transfers between devices  8.77 us (14%)
  matrix products  6.38 us (10%)
  local copies, waits for them, and re-layouts  3.31 us (5%)
  other arithmetic  3.1 us (5%)
    all_to_all x1, waiting for transfers between devices, dispatch(): lax.all_to_all(rows, 'expert', split_axis=0, concat_axis=0, tiled=True)  41.8 us
    all_to_all x1, starting transfers between devices, dispatch(): lax.all_to_all(rows, 'expert', split_axis=0, concat_axis=0, tiled=True)  7.56 us
    dot_general x1, matrix products, per_device(): lax.dot_general(received, w_down[0], (((1,), (1,)), ((), ())), preferred_...  6.38 us
    convert_element_type x1, other arithmetic, build_rows(): return rows.astype(jnp.bfloat16).reshape(pick.shape[1], most, grad.shape[1])  2.49 us
    gather x1, local copies, waits for them, and re-layouts, build_rows(): taken = jnp.take(grad, flat_ids, axis=0).astype(jnp.float32)  1.71 us
  transfers between devices with their start and end apart: 2, of which 2 were waited for; matrix products, arithmetic and copies ran while one was open for 3% of the time, Pallas kernels for 0%

commit v1 on v0

v1 whole, which is shorter than its diff:
```python
import functools

import jax
import jax.numpy as jnp
from jax import lax
from jax.experimental import pallas as pl
from jax.experimental.pallas import tpu as pltpu
from jax.sharding import PartitionSpec as P

CORE = 1
PAIR = 2
ROWS = 16
MIB = 1024 * 1024


def exchange(x, delta):
    peers = lax.axis_size("expert")
    return lax.ppermute(x, "expert", [(i, i ^ delta) for i in range(peers)])


def from_next_section(x, delta):
    sections, peers = lax.axis_size("section"), lax.axis_size("expert")
    pairs = [
        (s * peers + i, (s - 1) % sections * peers + (i ^ delta))
        for s in range(sections)
        for i in range(peers)
    ]
    return lax.ppermute(x, ("section", "expert"), pairs)


def assign_table(routes, gates, experts):
    match = routes[:, :, None] == jnp.arange(experts, dtype=jnp.int32)[None, None, :]
    table = jnp.sum(jnp.where(match, gates[:, :, None], 0.0), axis=1)
    high = lax.reduce_precision(table, exponent_bits=8, mantissa_bits=7)
    low = lax.reduce_precision(table - high, exponent_bits=8, mantissa_bits=7)
    return jnp.concatenate([high, low], axis=1).astype(jnp.bfloat16)


def with_tables(send, chunk, tables, delta):
    width = chunk.shape[1]
    keys = list(tables)
    got = send(jnp.concatenate([chunk] + [tables[k] for k in keys], axis=1))
    each = tables[keys[0]].shape[1]
    rest = {k ^ delta: got[:, width + n * each : width + (n + 1) * each] for n, k in enumerate(keys)}
    return got[:, :width], rest


def gather_tokens(grad, table):
    peers = lax.axis_size("expert")
    top = peers // 2
    far = from_next_section(grad, top)
    near = from_next_section(grad, 0)
    beside = from_next_section(grad, PAIR)
    tables = {0: table, top: exchange(table, top)}
    line = {0: near, top: far}
    delta = top // 2
    while delta > PAIR:
        held = list(line)
        for k in held[:-1]:
            line[k ^ delta] = exchange(line[k], delta)
        last = held[-1]
        line[last ^ delta], more = with_tables(
            functools.partial(exchange, delta=delta), line[last], tables, delta
        )
        tables = tables | more
        delta //= 2
    held = list(line)
    chunks = dict(line)
    chunks[PAIR] = beside
    for k in held[1:-1]:
        chunks[k ^ PAIR] = exchange(line[k], PAIR)
    last = held[-1]
    chunks[last ^ PAIR], more = with_tables(
        functools.partial(exchange, delta=PAIR), line[last], tables, PAIR
    )
    tables = tables | more
    return chunks, tables


def swap_cores(chunks, tables):
    keys = list(chunks)
    early, late = keys[: len(keys) // 2], keys[len(keys) // 2 :]
    groups = []
    first = exchange(jnp.concatenate([chunks[k] for k in early]), CORE)
    second = exchange(jnp.concatenate([chunks[k] for k in late]), CORE)
    names = list(tables)
    other = exchange(jnp.concatenate([tables[k] for k in names], axis=1), CORE)
    each = tables[names[0]].shape[1]
    for n, k in enumerate(names):
        tables = tables | {k ^ CORE: other[:, n * each : (n + 1) * each]}
    groups += [([k], chunks[k]) for k in keys]
    groups += [([k ^ CORE for k in early], first), ([k ^ CORE for k in late], second)]
    return groups, tables


def slot_units(order, most):
    blocks = max(1, ROWS // most)
    return blocks, list(dict.fromkeys(delta // blocks for delta in order))


def slot_bases(order, most, tok, me):
    blocks, units = slot_units(order, most)
    deltas = jnp.asarray(order, jnp.int32)
    starts = jnp.asarray([units.index(delta // blocks) * blocks * most for delta in order], jnp.int32)
    return jnp.repeat(starts + (me ^ deltas) % blocks * most, tok)[None, :]


def down_kernel(order, most, tok, *refs):
    me_ref, base_ref, table_ref, saved_ref, w_ref = refs[:5]
    token_refs, (out_ref, x_ref, d_ref) = refs[5:-3], refs[-3:]
    width = w_ref.shape[0]
    slots = saved_ref.shape[0]
    count = len(order) * tok
    blocks, units = slot_units(order, most)
    tall = blocks * most
    me = me_ref[0]
    at = 0
    for ref in token_refs:
        x_ref[at : at + ref.shape[0], :] = ref[...]
        at += ref.shape[0]
    experts = table_ref.shape[1] // 2
    lanes = lax.broadcasted_iota(jnp.int32, (8, 2 * experts), 1)
    pick = jnp.where((lanes == me) | (lanes == me + experts), 1.0, 0.0).astype(jnp.bfloat16)
    contract_last = (((1,), (1,)), ((), ()))
    gate = lax.dot_general(pick, table_ref[...], contract_last, preferred_element_type=jnp.float32)
    live = gate > 0.0
    rows = lax.broadcasted_iota(jnp.int32, (count, count), 0)
    cols = lax.broadcasted_iota(jnp.int32, (count, count), 1)
    earlier = jnp.where((rows < cols) & (rows // tok == cols // tok), 1.0, 0.0).astype(jnp.bfloat16)
    before = lax.dot_general(
        jnp.where(live, 1.0, 0.0).astype(jnp.bfloat16),
        earlier,
        (((1,), (0,)), ((), ())),
        preferred_element_type=jnp.float32,
    )
    slot = jnp.where(live[:1], base_ref[...] + before[:1].astype(jnp.int32), -1)
    hit = lax.broadcasted_iota(jnp.int32, (slots, count), 0) == slot
    weight = jnp.sum(jnp.where(hit, gate[:1], 0.0), axis=1, keepdims=True)
    onehot = jnp.where(hit, 1.0, 0.0).astype(jnp.bfloat16)
    step = 512 if x_ref.shape[1] % 512 == 0 else x_ref.shape[1]
    for k in range(0, x_ref.shape[1], step):
        taken = jnp.dot(onehot, x_ref[:, k : k + step], preferred_element_type=jnp.float32)
        d_ref[:, k : k + step] = (weight * taken).astype(jnp.bfloat16)
    wide = 256 if width % 256 == 0 else width
    for n in range(0, width, wide):
        hidden = lax.dot_general(
            d_ref[...], w_ref[n : n + wide, :], contract_last, preferred_element_type=jnp.float32
        )
        for i, delta in enumerate(units):
            place = pl.ds(pl.multiple_of((me // blocks ^ delta) * tall, tall), tall)
            h = hidden[i * tall : (i + 1) * tall]
            a = saved_ref[place, n : n + wide].astype(jnp.float32)
            u = saved_ref[place, width + n : width + n + wide].astype(jnp.float32)
            sig = jax.nn.sigmoid(a)
            hs = h * sig
            out_ref[place, n : n + wide] = (hs * u * (1.0 + a * (1.0 - sig))).astype(out_ref.dtype)
            out_ref[place, width + n : width + n + wide] = (hs * a).astype(out_ref.dtype)


def per_device(next_grad, routes, gates, saved, w_down):
    experts = lax.axis_size("expert")
    slots = saved.shape[2]
    most = slots // experts
    tok, features = next_grad.shape[1:]
    table = assign_table(routes[0], gates[0], experts)
    chunks, tables = gather_tokens(next_grad[0], table)
    groups, tables = swap_cores(chunks, tables)
    order = [k for keys, _ in groups for k in keys]
    table = jnp.concatenate([tables[k] for k in order])
    me = lax.axis_index("expert").astype(jnp.int32).reshape(1)
    vmem = pl.BlockSpec(memory_space=pltpu.VMEM)
    out = pl.pallas_call(
        functools.partial(down_kernel, order, most, tok),
        out_shape=jax.ShapeDtypeStruct(saved.shape[2:], jnp.bfloat16),
        in_specs=[pl.BlockSpec(memory_space=pltpu.SMEM)] + [vmem] * (4 + len(groups)),
        out_specs=vmem,
        scratch_shapes=[
            pltpu.VMEM((experts * tok, features), jnp.bfloat16),
            pltpu.VMEM((slots, features), jnp.bfloat16),
        ],
        compiler_params=pltpu.CompilerParams(vmem_limit_bytes=32 * MIB),
    )(me, slot_bases(order, most, tok, me), table, saved[0, 0], w_down[0], *[g for _, g in groups])
    return out[None, None]


def solution(mesh):
    return jax.shard_map(
        per_device,
        mesh=mesh,
        in_specs=(
            P("section", "expert", None),
            P("section", "expert", None),
            P("section", "expert", None),
            P("section", "expert", None, None),
            P("expert", None, None),
        ),
        out_specs=P("section", "expert", None, None),
        check_vma=False,
    )
```

time: 64.5 us -> 36.3 us (0.56)
  the two profiles are of different devices: /device:TPU:13 before, /device:TPU:0 now
where the time goes in v1:
time: 36.3 us; the launch traced here: 35.6 us
  starting transfers between devices  14.6 us (40%)
  waiting for transfers between devices  9.55 us (26%)
  local copies, waits for them, and re-layouts  7.12 us (20%)
  Pallas kernels  4.02 us (11%)
    ppermute x9, waiting for transfers between devices, exchange(): return lax.ppermute(x, 'expert', [(i, i ^ delta) for i in range(peers)])  9.16 us
    ppermute x3, starting transfers between devices, from_next_section(): return lax.ppermute(x, ('section', 'expert'), pairs)  8.25 us
    ppermute x9, starting transfers between devices, exchange(): return lax.ppermute(x, 'expert', [(i, i ^ delta) for i in range(peers)])  6.35 us
    unnamed x18, local copies, waits for them, and re-layouts  5.07 us
    pallas_call x1, Pallas kernels, per_device(): pl.pallas_call(functools.partial(down_kernel, order, most, tok), out_shap...  4.02 us
    eq x1, local copies, waits for them, and re-layouts, assign_table(): routes[:, :, None] == jnp.arange(experts, dtype=jnp.int32)[None, None, :]  0.76 us
    broadcast_in_dim x1, local copies, waits for them, and re-layouts, assign_table(): table = jnp.sum(jnp.where(match, gates[:, :, None], 0.0), axis=1)  0.76 us
  transfers between devices with their start and end apart: 12, of which 6 were waited for; matrix products, arithmetic and copies ran while one was open for 9% of the time, Pallas kernels for 0%

profile of v1, /device:TPU:0, one launch (start us, length us, event | category | flops | bytes accessed | tf_op | source)
XLA Modules:
  0.0 35.6 jit_solution(18371386111888014467)
XLA Ops:
  0.0 2.9 %collective-permute-start.5 = (bf16[16,3584]{1,0:T(8,128)(2,1)}, bf16[16,3584]{1,0:T(8,128)(2,1)S(1)}, u32[]{:S(2)}, u32[]{:S(2)}) collective-permute-start(bf16[16,3584]{1,0:T(8,128)(2,1)} %bitcast.11), channel_id=1, source_target_pairs={{0,16},{1,17},{2,18},{3,19},{4,20},{5,21},{6,22},{7,23},{8,24},{9,... | collective-permute-start | bytes 344072 | tf_op jit(solution)/shard_map/ppermute | solution.py:28
  2.9 2.6 %collective-permute-start.1 = (bf16[16,3584]{1,0:T(8,128)(2,1)}, bf16[16,3584]{1,0:T(8,128)(2,1)S(1)}, u32[]{:S(2)}, u32[]{:S(2)}) collective-permute-start(bf16[16,3584]{1,0:T(8,128)(2,1)} %bitcast.12), channel_id=1, source_target_pairs={{0,24},{1,25},{2,26},{3,27},{4,28},{5,29},{6,30},{7,31},{8,16},{9,... | collective-permute-start | bytes 344072 | tf_op jit(solution)/shard_map/ppermute | solution.py:28
  5.5 0.8 %copy.28 = s32[16,8]{1,0:T(8,128)S(1)} copy(s32[16,8]{0,1:T(8,128)} %bitcast.9) | data formatting | bytes 1024 | tf_op jit(solution)/shard_map/eq | solution.py:32
  6.3 0.8 %copy.29 = f32[16,8]{1,0:T(8,128)S(1)} copy(f32[16,8]{0,1:T(8,128)} %bitcast.10) | data formatting | bytes 1024 | tf_op jit(solution)/shard_map/jit(_where)/broadcast_in_dim | solution.py:33
  7.0 0.1 select_reduce_fusion
  7.1 0.1 constant_dynamic-update-slice_fusion.15
  7.2 0.0 collective-permute-start
  7.3 2.8 %collective-permute-start.7 = (bf16[16,3584]{1,0:T(8,128)(2,1)}, bf16[16,3584]{1,0:T(8,128)(2,1)S(1)}, u32[]{:S(2)}, u32[]{:S(2)}) collective-permute-start(bf16[16,3584]{1,0:T(8,128)(2,1)} %bitcast.13), channel_id=1, source_target_pairs={{0,18},{1,19},{2,16},{3,17},{4,22},{5,23},{6,20},{7,21},{8,26},{9,... | collective-permute-start | bytes 344072 | tf_op jit(solution)/shard_map/ppermute | solution.py:28
  10.0 1.7 %collective-permute-done = bf16[16,32]{1,0:T(8,128)(2,1)S(1)} collective-permute-done((bf16[16,32]{1,0:T(8,128)(2,1)S(1)}, bf16[16,32]{1,0:T(8,128)(2,1)S(1)}, u32[]{:S(2)}, u32[]{:S(2)}) %collective-permute-start) | collective-permute-done | bytes 1056 | tf_op jit(solution)/shard_map/ppermute | solution.py:18
  11.7 0.4 %collective-permute-done.1.refs_6_ = bf16[16,3584]{1,0:T(8,128)(2,1)S(1)} collective-permute-done((bf16[16,3584]{1,0:T(8,128)(2,1)}, bf16[16,3584]{1,0:T(8,128)(2,1)S(1)}, u32[]{:S(2)}, u32[]{:S(2)}) %collective-permute-start.1) | collective-permute-done | bytes 114720 | tf_op jit(solution)/shard_map/ppermute | solution.py:28
  12.1 0.1 concatenate.28
  12.2 1.2 %collective-permute-start.2 = (bf16[16,3648]{1,0:T(8,128)(2,1)S(1)}, bf16[16,3648]{1,0:T(8,128)(2,1)S(1)}, u32[]{:S(2)}, u32[]{:S(2)}) collective-permute-start(bf16[16,3648]{1,0:T(8,128)(2,1)S(1)} %concatenate.28), channel_id=1, source_target_pairs={{0,4},{1,5},{2,6},{3,7},{4,0},{5,1},{6,2},{7,3},{8,12},{9,13},{10,... | collective-permute-start | bytes 350216 | tf_op jit(solution)/shard_map/ppermute | solution.py:18
  13.4 0.0 collective-permute-done.5.refs_5_
  13.4 0.8 %collective-permute-start.6 = (bf16[16,3584]{1,0:T(8,128)(2,1)S(1)}, bf16[16,3584]{1,0:T(8,128)(2,1)S(1)}, u32[]{:S(2)}, u32[]{:S(2)}) collective-permute-start(bf16[16,3584]{1,0:T(8,128)(2,1)S(1)} %collective-permute-done.5.refs_5_), channel_id=1, source_target_pairs={{0,4},{1,5},{2,6},{3,7},{4,0},{5,1},{6,2},{7,3},{8,12},{9,13},{10,... | collective-permute-start | bytes 344072 | tf_op jit(solution)/shard_map/ppermute | solution.py:18
  14.2 0.1 broadcast_in_dim.21
  14.3 0.1 broadcast_in_dim_reshape.3.refs_1_
  14.4 1.6 %collective-permute-start.8 = (bf16[16,3584]{1,0:T(8,128)(2,1)S(1)}, bf16[16,3584]{1,0:T(8,128)(2,1)S(1)}, u32[]{:S(2)}, u32[]{:S(2)}) collective-permute-start(bf16[16,3584]{1,0:T(8,128)(2,1)S(1)} %collective-permute-done.1.refs_6_), channel_id=1, source_target_pairs={{0,2},{1,3},{2,0},{3,1},{4,6},{5,7},{6,4},{7,5},{8,10},{9,11},{10,... | collective-permute-start | bytes 344072 | tf_op jit(solution)/shard_map/ppermute | solution.py:18
  16.0 2.6 %collective-permute-done.6.refs_7_ = bf16[16,3584]{1,0:T(8,128)(2,1)S(1)} collective-permute-done((bf16[16,3584]{1,0:T(8,128)(2,1)S(1)}, bf16[16,3584]{1,0:T(8,128)(2,1)S(1)}, u32[]{:S(2)}, u32[]{:S(2)}) %collective-permute-start.6) | collective-permute-done | bytes 114720 | tf_op jit(solution)/shard_map/ppermute | solution.py:18
  18.7 1.5 %collective-permute-start.9 = (bf16[16,3584]{1,0:T(8,128)(2,1)S(1)}, bf16[16,3584]{1,0:T(8,128)(2,1)S(1)}, u32[]{:S(2)}, u32[]{:S(2)}) collective-permute-start(bf16[16,3584]{1,0:T(8,128)(2,1)S(1)} %collective-permute-done.6.refs_7_), channel_id=1, source_target_pairs={{0,2},{1,3},{2,0},{3,1},{4,6},{5,7},{6,4},{7,5},{8,10},{9,11},{10,... | collective-permute-start | bytes 344072 | tf_op jit(solution)/shard_map/ppermute | solution.py:18
  20.2 0.0 collective-permute-done.2
  20.2 0.1 concatenate.29
  20.3 0.5 %collective-permute-start.3 = (bf16[16,3712]{1,0:T(8,128)(2,1)S(1)}, bf16[16,3712]{1,0:T(8,128)(2,1)S(1)}, u32[]{:S(2)}, u32[]{:S(2)}) collective-permute-start(bf16[16,3712]{1,0:T(8,128)(2,1)S(1)} %concatenate.29), channel_id=1, source_target_pairs={{0,2},{1,3},{2,0},{3,1},{4,6},{5,7},{6,4},{7,5},{8,10},{9,11},{10,... | collective-permute-start | bytes 356360 | tf_op jit(solution)/shard_map/ppermute | solution.py:18
  20.8 0.1 collective-permute-start.10
  20.9 0.1 constant_dynamic-update-slice_fusion.12
  21.0 4.1 %collective-permute-done.3 = bf16[16,3712]{1,0:T(8,128)(2,1)S(1)} collective-permute-done((bf16[16,3712]{1,0:T(8,128)(2,1)S(1)}, bf16[16,3712]{1,0:T(8,128)(2,1)S(1)}, u32[]{:S(2)}, u32[]{:S(2)}) %collective-permute-start.3) | collective-permute-done | bytes 118816 | tf_op jit(solution)/shard_map/ppermute | solution.py:18
  25.1 0.1 concatenate.30
  25.2 0.0 collective-permute-start.4
  25.2 0.0 collective-permute-done.7.refs_9_
  25.3 0.0 collective-permute-done.8.refs_10_
  25.3 0.0 collective-permute-done.9.refs_11_
  25.3 0.6 %collective-permute-start.11 = (bf16[64,3584]{1,0:T(8,128)(2,1)S(1)}, bf16[64,3584]{1,0:T(8,128)(2,1)S(1)}, u32[]{:S(2)}, u32[]{:S(2)}) collective-permute-start(bf16[64,3584]{1,0:T(8,128)(2,1)S(1)} %pad_maximum_fusion.1), channel_id=1, source_target_pairs={{0,1},{1,0},{2,3},{3,2},{4,5},{5,4},{6,7},{7,6},{8,9},{9,8},{10,11... | collective-permute-start | bytes 1376264 | tf_op jit(solution)/shard_map/ppermute | solution.py:18
  25.9 0.1 constant_dynamic-update-slice_fusion.10
  26.0 0.1 constant_dynamic-update-slice_fusion.9
  26.0 0.1 constant_dynamic-update-slice_fusion.8
  26.1 0.3 collective-permute-done.4
  26.4 0.1 constant_dynamic-update-slice_fusion.6
  26.5 0.1 constant_dynamic-update-slice_fusion.5
  26.6 0.1 constant_dynamic-update-slice_fusion.4
  26.6 0.1 constant_dynamic-update-slice_fusion.2
  26.7 0.1 constant_dynamic-update-slice_fusion.1
  26.8 0.1 constant_dynamic-update-slice_fusion.refs_2_
  26.9 0.0 collective-permute-done.10.refs_13_
  26.9 0.4 %collective-permute-done.11.refs_14_ = bf16[64,3584]{1,0:T(8,128)(2,1)S(1)} collective-permute-done((bf16[64,3584]{1,0:T(8,128)(2,1)S(1)}, bf16[64,3584]{1,0:T(8,128)(2,1)S(1)}, u32[]{:S(2)}, u32[]{:S(2)}) %collective-permute-start.11) | collective-permute-done | bytes 458784 | tf_op jit(solution)/shard_map/ppermute | solution.py:18
  27.3 0.0 copy-start
  27.3 3.1 %copy-done = bf16[1,1024,3584]{2,1,0:T(8,128)(2,1)S(1)} copy-done((bf16[1,1024,3584]{2,1,0:T(8,128)(2,1)S(1)}, bf16[1,1024,3584]{2,1,0:T(8,128)(2,1)}, u32[]{:S(2)}) %copy-start) | copy-done | bytes 7340056
  30.4 0.0 copy-start.1
  30.4 1.2 %copy-done.1 = bf16[1,1,256,2048]{3,2,1,0:T(8,128)(2,1)S(1)} copy-done((bf16[1,1,256,2048]{3,2,1,0:T(8,128)(2,1)S(1)}, bf16[1,1,256,2048]{3,2,1,0:T(8,128)(2,1)}, u32[]{:S(2)}) %copy-start.1) | copy-done | bytes 1048600
  31.6 4.0 %shard_map.69 = bf16[256,2048]{1,0:T(8,128)(2,1)} custom-call(s32[1]{0:T(128)} %bitcast.refs_0_, s32[1,256]{1,0:T(1,128)S(1)} %broadcast_in_dim_reshape.3.refs_1_, bf16[256,32]{1,0:T(8,128)(2,1)S(1)} %constant_dynamic-update-slice_fusion.refs_2_, bf16[256,2048]{1,0:T(8,128)(2,1)S(1)} %bitcast.8, bf16[1024,3584]{1,0:T(8,128)(2,1)S(1)} %bitcast.7, ...), custom_call_target="tpu_custom_call" | custom-call | tf_op jit(solution)/shard_map/pallas_call | solution.py:172
  (13 shorter events, 0.1 us)
Async XLA Ops:
  0.0 13.4 %collective-permute-start.5 = (bf16[16,3584]{1,0:T(8,128)(2,1)}, bf16[16,3584]{1,0:T(8,128)(2,1)S(1)}, u32[]{:S(2)}, u32[]{:S(2)}) collective-permute-start(bf16[16,3584]{1,0:T(8,128)(2,1)} %bitcast.11), channel_id=1, source_target_pairs={{0,16},{1,17},{2,18},{3,19},{4,20},{5,21},{6,22},{7,23},{8,24},{9,... | collective-permute-start | bytes 344072 | tf_op jit(solution)/shard_map/ppermute | solution.py:28
  2.9 9.2 %collective-permute-start.1 = (bf16[16,3584]{1,0:T(8,128)(2,1)}, bf16[16,3584]{1,0:T(8,128)(2,1)S(1)}, u32[]{:S(2)}, u32[]{:S(2)}) collective-permute-start(bf16[16,3584]{1,0:T(8,128)(2,1)} %bitcast.12), channel_id=1, source_target_pairs={{0,24},{1,25},{2,26},{3,27},{4,28},{5,29},{6,30},{7,31},{8,16},{9,... | collective-permute-start | bytes 344072 | tf_op jit(solution)/shard_map/ppermute | solution.py:28
  7.2 4.5 %collective-permute-start = (bf16[16,32]{1,0:T(8,128)(2,1)S(1)}, bf16[16,32]{1,0:T(8,128)(2,1)S(1)}, u32[]{:S(2)}, u32[]{:S(2)}) collective-permute-start(bf16[16,32]{1,0:T(8,128)(2,1)S(1)} %get-tuple-element.6), channel_id=1, source_target_pairs={{0,8},{1,9},{2,10},{3,11},{4,12},{5,13},{6,14},{7,15},{8,0},{9,1},... | collective-permute-start | bytes 3080 | tf_op jit(solution)/shard_map/ppermute | solution.py:18
  7.3 18.0 %collective-permute-start.7 = (bf16[16,3584]{1,0:T(8,128)(2,1)}, bf16[16,3584]{1,0:T(8,128)(2,1)S(1)}, u32[]{:S(2)}, u32[]{:S(2)}) collective-permute-start(bf16[16,3584]{1,0:T(8,128)(2,1)} %bitcast.13), channel_id=1, source_target_pairs={{0,18},{1,19},{2,16},{3,17},{4,22},{5,23},{6,20},{7,21},{8,26},{9,... | collective-permute-start | bytes 344072 | tf_op jit(solution)/shard_map/ppermute | solution.py:28
  12.2 8.0 %collective-permute-start.2 = (bf16[16,3648]{1,0:T(8,128)(2,1)S(1)}, bf16[16,3648]{1,0:T(8,128)(2,1)S(1)}, u32[]{:S(2)}, u32[]{:S(2)}) collective-permute-start(bf16[16,3648]{1,0:T(8,128)(2,1)S(1)} %concatenate.28), channel_id=1, source_target_pairs={{0,4},{1,5},{2,6},{3,7},{4,0},{5,1},{6,2},{7,3},{8,12},{9,13},{10,... | collective-permute-start | bytes 350216 | tf_op jit(solution)/shard_map/ppermute | solution.py:18
  13.4 5.2 %collective-permute-start.6 = (bf16[16,3584]{1,0:T(8,128)(2,1)S(1)}, bf16[16,3584]{1,0:T(8,128)(2,1)S(1)}, u32[]{:S(2)}, u32[]{:S(2)}) collective-permute-start(bf16[16,3584]{1,0:T(8,128)(2,1)S(1)} %collective-permute-done.5.refs_5_), channel_id=1, source_target_pairs={{0,4},{1,5},{2,6},{3,7},{4,0},{5,1},{6,2},{7,3},{8,12},{9,13},{10,... | collective-permute-start | bytes 344072 | tf_op jit(solution)/shard_map/ppermute | solution.py:18
  14.4 10.9 %collective-permute-start.8 = (bf16[16,3584]{1,0:T(8,128)(2,1)S(1)}, bf16[16,3584]{1,0:T(8,128)(2,1)S(1)}, u32[]{:S(2)}, u32[]{:S(2)}) collective-permute-start(bf16[16,3584]{1,0:T(8,128)(2,1)S(1)} %collective-permute-done.1.refs_6_), channel_id=1, source_target_pairs={{0,2},{1,3},{2,0},{3,1},{4,6},{5,7},{6,4},{7,5},{8,10},{9,11},{10,... | collective-permute-start | bytes 344072 | tf_op jit(solution)/shard_map/ppermute | solution.py:18
  18.7 6.6 %collective-permute-start.9 = (bf16[16,3584]{1,0:T(8,128)(2,1)S(1)}, bf16[16,3584]{1,0:T(8,128)(2,1)S(1)}, u32[]{:S(2)}, u32[]{:S(2)}) collective-permute-start(bf16[16,3584]{1,0:T(8,128)(2,1)S(1)} %collective-permute-done.6.refs_7_), channel_id=1, source_target_pairs={{0,2},{1,3},{2,0},{3,1},{4,6},{5,7},{6,4},{7,5},{8,10},{9,11},{10,... | collective-permute-start | bytes 344072 | tf_op jit(solution)/shard_map/ppermute | solution.py:18
  20.3 4.8 %collective-permute-start.3 = (bf16[16,3712]{1,0:T(8,128)(2,1)S(1)}, bf16[16,3712]{1,0:T(8,128)(2,1)S(1)}, u32[]{:S(2)}, u32[]{:S(2)}) collective-permute-start(bf16[16,3712]{1,0:T(8,128)(2,1)S(1)} %concatenate.29), channel_id=1, source_target_pairs={{0,2},{1,3},{2,0},{3,1},{4,6},{5,7},{6,4},{7,5},{8,10},{9,11},{10,... | collective-permute-start | bytes 356360 | tf_op jit(solution)/shard_map/ppermute | solution.py:18
  20.8 6.1 %collective-permute-start.10 = (bf16[64,3584]{1,0:T(8,128)(2,1)S(1)}, bf16[64,3584]{1,0:T(8,128)(2,1)S(1)}, u32[]{:S(2)}, u32[]{:S(2)}) collective-permute-start(bf16[64,3584]{1,0:T(8,128)(2,1)S(1)} %pad_maximum_fusion), channel_id=1, source_target_pairs={{0,1},{1,0},{2,3},{3,2},{4,5},{5,4},{6,7},{7,6},{8,9},{9,8},{10,11... | collective-permute-start | bytes 1376264 | tf_op jit(solution)/shard_map/ppermute | solution.py:18
  25.2 1.2 %collective-permute-start.4 = (bf16[16,256]{1,0:T(8,128)(2,1)S(1)}, bf16[16,256]{1,0:T(8,128)(2,1)S(1)}, u32[]{:S(2)}, u32[]{:S(2)}) collective-permute-start(bf16[16,256]{1,0:T(8,128)(2,1)S(1)} %concatenate.30), channel_id=1, source_target_pairs={{0,1},{1,0},{2,3},{3,2},{4,5},{5,4},{6,7},{7,6},{8,9},{9,8},{10,11... | collective-permute-start | bytes 24584 | tf_op jit(solution)/shard_map/ppermute | solution.py:18
  25.3 2.0 %collective-permute-start.11 = (bf16[64,3584]{1,0:T(8,128)(2,1)S(1)}, bf16[64,3584]{1,0:T(8,128)(2,1)S(1)}, u32[]{:S(2)}, u32[]{:S(2)}) collective-permute-start(bf16[64,3584]{1,0:T(8,128)(2,1)S(1)} %pad_maximum_fusion.1), channel_id=1, source_target_pairs={{0,1},{1,0},{2,3},{3,2},{4,5},{5,4},{6,7},{7,6},{8,9},{9,8},{10,11... | collective-permute-start | bytes 1376264 | tf_op jit(solution)/shard_map/ppermute | solution.py:18
  27.3 3.1 %copy-start = (bf16[1,1024,3584]{2,1,0:T(8,128)(2,1)S(1)}, bf16[1,1024,3584]{2,1,0:T(8,128)(2,1)}, u32[]{:S(2)}) copy-start(bf16[1,1024,3584]{2,1,0:T(8,128)(2,1)} %param.10) | copy-start | bytes 22020100
  30.4 1.2 %copy-start.1 = (bf16[1,1,256,2048]{3,2,1,0:T(8,128)(2,1)S(1)}, bf16[1,1,256,2048]{3,2,1,0:T(8,128)(2,1)}, u32[]{:S(2)}) copy-start(bf16[1,1,256,2048]{3,2,1,0:T(8,128)(2,1)} %param.9) | copy-start | bytes 3145732

commit v2 on v1

v2 whole, which is shorter than its diff:
```python
import functools

import jax
import jax.numpy as jnp
from jax import lax
from jax.experimental import pallas as pl
from jax.experimental.pallas import tpu as pltpu
from jax.sharding import PartitionSpec as P

in_space = pltpu.with_memory_space_constraint

CORE = 1
PAIR = 2
ROWS = 16
W_PARTS = 4
W_LOADS = 8
MIB = 1024 * 1024


def exchange(x, delta):
    peers = lax.axis_size("expert")
    return lax.ppermute(x, "expert", [(i, i ^ delta) for i in range(peers)])


def from_next_section(x, delta):
    sections, peers = lax.axis_size("section"), lax.axis_size("expert")
    pairs = [
        (s * peers + i, (s - 1) % sections * peers + (i ^ delta))
        for s in range(sections)
        for i in range(peers)
    ]
    return lax.ppermute(x, ("section", "expert"), pairs)


def table_kernel(routes_ref, gates_ref, out_ref):
    tok, experts = out_ref.shape[0], out_ref.shape[1] // 2
    ids = lax.broadcasted_iota(jnp.int32, (tok, experts), 1)
    table = jnp.zeros((tok, experts), jnp.float32)
    for k in range(routes_ref.shape[1]):
        table += jnp.where(routes_ref[:, k : k + 1] == ids, gates_ref[:, k : k + 1], 0.0)
    high = table.astype(jnp.bfloat16)
    out_ref[:, :experts] = high
    out_ref[:, experts:] = (table - high.astype(jnp.float32)).astype(jnp.bfloat16)


def assign_table(routes, gates, experts):
    vmem = pl.BlockSpec(memory_space=pltpu.VMEM)
    return pl.pallas_call(
        table_kernel,
        out_shape=jax.ShapeDtypeStruct((routes.shape[0], 2 * experts), jnp.bfloat16),
        in_specs=[vmem, vmem],
        out_specs=vmem,
        compiler_params=pltpu.CompilerParams(vmem_limit_bytes=MIB),
    )(routes, gates)


def with_tables(send, chunk, tables, delta):
    width = chunk.shape[1]
    keys = list(tables)
    got = send(jnp.concatenate([chunk] + [tables[k] for k in keys], axis=1))
    each = tables[keys[0]].shape[1]
    rest = {k ^ delta: got[:, width + n * each : width + (n + 1) * each] for n, k in enumerate(keys)}
    return got[:, :width], rest


def gather_tokens(grad, table):
    peers = lax.axis_size("expert")
    top = peers // 2
    far, near = from_next_section(grad, top), from_next_section(grad, 0)
    beside = from_next_section(grad, PAIR)
    tables = {0: table, top: exchange(table, top)}
    chunks = {0: near, top: far}
    delta = top // 2
    while delta > PAIR:
        held = list(chunks)
        for k in held:
            if k == 0:
                chunks[k ^ delta], more = with_tables(
                    functools.partial(exchange, delta=delta), chunks[k], tables, delta
                )
            else:
                chunks[k ^ delta] = exchange(chunks[k], delta)
        tables = tables | more
        delta //= 2
    line = list(chunks)
    chunks[PAIR] = beside
    for k in line[1:]:
        if k == 4:
            chunks[k ^ PAIR], more = with_tables(
                functools.partial(exchange, delta=PAIR), chunks[k], tables, PAIR
            )
        else:
            chunks[k ^ PAIR] = exchange(chunks[k], PAIR)
    return chunks, tables | more


def swap_cores(chunks, tables, early):
    late = [k for k in chunks if k not in early]
    groups = []
    for part in (early, late):
        own = jnp.concatenate([chunks[k] for k in part])
        groups += [(part, own), ([k ^ CORE for k in part], exchange(own, CORE))]
    names = list(tables)
    own = jnp.concatenate([tables[k] for k in names], axis=1)
    return groups, [(names, own), ([k ^ CORE for k in names], exchange(own, CORE))]


def slot_units(order, most):
    blocks = max(1, ROWS // most)
    return blocks, list(dict.fromkeys(delta // blocks for delta in order))


def slot_bases(order, most, tok, me):
    blocks, units = slot_units(order, most)
    deltas = jnp.asarray(order, jnp.int32)
    starts = jnp.asarray([units.index(delta // blocks) * blocks * most for delta in order], jnp.int32)
    return jnp.repeat(starts + (me ^ deltas) % blocks * most, tok)[None, :]


def down_kernel(order, table_order, most, tok, *refs):
    me_ref, base_ref, saved_hbm, w_hbm = refs[:4]
    table_refs = refs[4 : 4 + len(table_order)]
    token_refs = refs[4 + len(table_order) : -7]
    out_ref, x_ref, d_ref, table_ref, saved_ref, w_ref, sems = refs[-7:]
    width = w_ref.shape[0]
    slots = saved_ref.shape[0]
    count = len(order) * tok
    blocks, units = slot_units(order, most)
    tall = blocks * most
    me = me_ref[0]
    height = width // W_LOADS

    def load(n):
        part = pl.ds(pl.multiple_of(n * height, height), height)
        return pltpu.make_async_copy(w_hbm.at[part], w_ref.at[part], sems.at[n])

    saved_load = pltpu.make_async_copy(saved_hbm, saved_ref, sems.at[W_LOADS])
    for n in range(W_LOADS):
        load(n).start()
        if n == 0:
            saved_load.start()
    at = 0
    for ref in token_refs:
        x_ref[at : at + ref.shape[0], :] = ref[...]
        at += ref.shape[0]
    experts = table_ref.shape[1] // 2
    for names, ref in zip(table_order, table_refs, strict=True):
        for n, k in enumerate(names):
            i = order.index(k)
            table_ref[i * tok : (i + 1) * tok, :] = ref[:, n * 2 * experts : (n + 1) * 2 * experts]
    lanes = lax.broadcasted_iota(jnp.int32, (8, 2 * experts), 1)
    pick = jnp.where((lanes == me) | (lanes == me + experts), 1.0, 0.0).astype(jnp.bfloat16)
    contract_last = (((1,), (1,)), ((), ()))
    gate = lax.dot_general(pick, table_ref[...], contract_last, preferred_element_type=jnp.float32)
    live = gate > 0.0
    rows = lax.broadcasted_iota(jnp.int32, (count, count), 0)
    cols = lax.broadcasted_iota(jnp.int32, (count, count), 1)
    earlier = jnp.where((rows < cols) & (rows // tok == cols // tok), 1.0, 0.0).astype(jnp.bfloat16)
    before = lax.dot_general(
        jnp.where(live, 1.0, 0.0).astype(jnp.bfloat16),
        earlier,
        (((1,), (0,)), ((), ())),
        preferred_element_type=jnp.float32,
    )
    slot = jnp.where(live[:1], base_ref[...] + before[:1].astype(jnp.int32), -1)
    hit = lax.broadcasted_iota(jnp.int32, (slots, count), 0) == slot
    weight = jnp.sum(jnp.where(hit, gate[:1], 0.0), axis=1, keepdims=True)
    onehot = jnp.where(hit, 1.0, 0.0).astype(jnp.bfloat16)
    step = 512 if x_ref.shape[1] % 512 == 0 else x_ref.shape[1]
    for k in range(0, x_ref.shape[1], step):
        taken = jnp.dot(onehot, x_ref[:, k : k + step], preferred_element_type=jnp.float32)
        d_ref[:, k : k + step] = (weight * taken).astype(jnp.bfloat16)
    saved_load.wait()
    wide = width // W_PARTS

    @pl.loop(0, W_PARTS)
    def _(part):
        for n in range(W_LOADS // W_PARTS):
            load(part * (W_LOADS // W_PARTS) + n).wait()
        at = pl.multiple_of(part * wide, wide)
        hidden = lax.dot_general(
            d_ref[...], w_ref[pl.ds(at, wide), :], contract_last, preferred_element_type=jnp.float32
        )
        for i, delta in enumerate(units):
            place = pl.ds(pl.multiple_of((me // blocks ^ delta) * tall, tall), tall)
            h = hidden[i * tall : (i + 1) * tall]
            a = saved_ref[place, pl.ds(at, wide)].astype(jnp.float32)
            u = saved_ref[place, pl.ds(width + at, wide)].astype(jnp.float32)
            sig = jax.nn.sigmoid(a)
            hs = h * sig
            out_ref[place, pl.ds(at, wide)] = (hs * u * (1.0 + a * (1.0 - sig))).astype(out_ref.dtype)
            out_ref[place, pl.ds(width + at, wide)] = (hs * a).astype(out_ref.dtype)


def per_device(next_grad, routes, gates, saved, w_down):
    experts = lax.axis_size("expert")
    most = saved.shape[2] // experts
    tok, features = next_grad.shape[1:]
    table = assign_table(routes[0], gates[0], experts)
    chunks, tables = gather_tokens(next_grad[0], table)
    groups, tables = swap_cores(chunks, tables, [0, 8, 4, 2, 10])
    order = [k for keys, _ in groups for k in keys]
    me = lax.axis_index("expert").astype(jnp.int32).reshape(1)
    vmem, hbm = pl.BlockSpec(memory_space=pltpu.VMEM), pl.BlockSpec(memory_space=pl.ANY)
    out = pl.pallas_call(
        functools.partial(down_kernel, order, [names for names, _ in tables], most, tok),
        out_shape=jax.ShapeDtypeStruct(saved.shape[2:], jnp.bfloat16),
        in_specs=[pl.BlockSpec(memory_space=pltpu.SMEM), vmem, hbm, hbm]
        + [vmem] * (len(tables) + len(groups)),
        out_specs=vmem,
        scratch_shapes=[
            pltpu.VMEM((experts * tok, features), jnp.bfloat16),
            pltpu.VMEM((saved.shape[2], features), jnp.bfloat16),
            pltpu.VMEM((experts * tok, 2 * experts), jnp.bfloat16),
            pltpu.VMEM(saved.shape[2:], jnp.bfloat16),
            pltpu.VMEM(w_down.shape[1:], jnp.bfloat16),
            pltpu.SemaphoreType.DMA((W_LOADS + 1,)),
        ],
        compiler_params=pltpu.CompilerParams(vmem_limit_bytes=40 * MIB),
    )(
        me,
        slot_bases(order, most, tok, me),
        in_space(saved[0, 0], pltpu.HBM),
        in_space(w_down[0], pltpu.HBM),
        *[t for _, t in tables],
        *[g for _, g in groups],
    )
    return out[None, None]


def solution(mesh):
    return jax.shard_map(
        per_device,
        mesh=mesh,
        in_specs=(
            P("section", "expert", None),
            P("section", "expert", None),
            P("section", "expert", None),
            P("section", "expert", None, None),
            P("expert", None, None),
        ),
        out_specs=P("section", "expert", None, None),
        check_vma=False,
    )
```

time: 36.3 us -> 33 us (0.909); the launches traced: 35.6 us -> 32.8 us
  local copies, waits for them, and re-layouts: 7.12 us -> 1.92 us
  Pallas kernels: 4.02 us -> 6.56 us
    unnamed x18 -> x4, local copies, waits for them, and re-layouts: 5.07 us -> 0.04 us
    pallas_call x1 -> x2, Pallas kernels: 4.02 us -> 6.56 us  [the longest x1 6.38 us: per_device(): pl.pallas_call(functools.partial(down_kernel, order, [names for names, _...]
    squeeze x0 -> x2, local copies, waits for them, and re-layouts: none -> 1.51 us  [per_device(): table = assign_table(routes[0], gates[0], experts)]
    broadcast_in_dim x1 -> x0, local copies, waits for them, and re-layouts: 0.76 us -> none  [assign_table(): table = jnp.sum(jnp.where(match, gates[:, :, None], 0.0), axis=1)]
    eq x1 -> x0, local copies, waits for them, and re-layouts: 0.76 us -> none  [assign_table(): routes[:, :, None] == jnp.arange(experts, dtype=jnp.int32)[None, None, :]]
    ppermute x9, waiting for transfers between devices: 9.16 us -> 9.64 us  [exchange(): return lax.ppermute(x, 'expert', [(i, i ^ delta) for i in range(peers)])]
    ppermute x3, waiting for transfers between devices: 0.38 us -> 0.01 us  [from_next_section(): return lax.ppermute(x, ('section', 'expert'), pairs)]
  transfers between devices with their start and end apart: 12 -> 12, of which waited for: 6 -> 4; matrix products, arithmetic and copies ran while one was open for 9% -> 6% of each run, Pallas kernels for 0% -> 1%
where the time goes in v2:
time: 33 us; the launch traced here: 32.8 us
  starting transfers between devices  14.5 us (44%)
  waiting for transfers between devices  9.65 us (29%)
  Pallas kernels  6.56 us (20%)
  local copies, waits for them, and re-layouts  1.92 us (6%)
    ppermute x9, waiting for transfers between devices, exchange(): return lax.ppermute(x, 'expert', [(i, i ^ delta) for i in range(peers)])  9.64 us
    ppermute x3, starting transfers between devices, from_next_section(): return lax.ppermute(x, ('section', 'expert'), pairs)  8.25 us
    pallas_call x1, Pallas kernels, per_device(): pl.pallas_call(functools.partial(down_kernel, order, [names for names, _...  6.38 us
    ppermute x9, starting transfers between devices, exchange(): return lax.ppermute(x, 'expert', [(i, i ^ delta) for i in range(peers)])  6.25 us
    squeeze x2, local copies, waits for them, and re-layouts, per_device(): table = assign_table(routes[0], gates[0], experts)  1.51 us
  transfers between devices with their start and end apart: 12, of which 4 were waited for; matrix products, arithmetic and copies ran while one was open for 6% of the time, Pallas kernels for 1%

profile of v2, /device:TPU:0, one launch (start us, length us, event | category | flops | bytes accessed | tf_op | source)
XLA Modules:
  0.0 32.8 jit_solution(7587574187939381696)
XLA Ops:
  0.0 2.9 %collective-permute-start.1 = (bf16[16,3584]{1,0:T(8,128)(2,1)}, bf16[16,3584]{1,0:T(8,128)(2,1)S(1)}, u32[]{:S(2)}, u32[]{:S(2)}) collective-permute-start(bf16[16,3584]{1,0:T(8,128)(2,1)} %bitcast.11), channel_id=1, source_target_pairs={{0,16},{1,17},{2,18},{3,19},{4,20},{5,21},{6,22},{7,23},{8,24},{9,... | collective-permute-start | bytes 344072 | tf_op jit(solution)/shard_map/ppermute | solution.py:32
  2.9 2.6 %collective-permute-start.5 = (bf16[16,3584]{1,0:T(8,128)(2,1)}, bf16[16,3584]{1,0:T(8,128)(2,1)S(1)}, u32[]{:S(2)}, u32[]{:S(2)}) collective-permute-start(bf16[16,3584]{1,0:T(8,128)(2,1)} %bitcast.12), channel_id=1, source_target_pairs={{0,24},{1,25},{2,26},{3,27},{4,28},{5,29},{6,30},{7,31},{8,16},{9,... | collective-permute-start | bytes 344072 | tf_op jit(solution)/shard_map/ppermute | solution.py:32
  5.5 0.8 %copy.7.routes_ref = s32[16,8]{1,0:T(8,128)S(1)} copy(s32[16,8]{0,1:T(8,128)} %bitcast.9) | data formatting | bytes 1024 | tf_op jit(solution)/shard_map/squeeze | solution.py:199
  6.3 0.8 %copy.8.gates_ref = f32[16,8]{1,0:T(8,128)S(1)} copy(f32[16,8]{0,1:T(8,128)} %bitcast.10) | data formatting | bytes 1024 | tf_op jit(solution)/shard_map/squeeze | solution.py:199
  7.0 0.2 shard_map.69
  7.2 0.0 collective-permute-start
  7.2 2.8 %collective-permute-start.6 = (bf16[16,3584]{1,0:T(8,128)(2,1)}, bf16[16,3584]{1,0:T(8,128)(2,1)S(1)}, u32[]{:S(2)}, u32[]{:S(2)}) collective-permute-start(bf16[16,3584]{1,0:T(8,128)(2,1)} %bitcast.13), channel_id=1, source_target_pairs={{0,18},{1,19},{2,16},{3,17},{4,22},{5,23},{6,20},{7,21},{8,26},{9,... | collective-permute-start | bytes 344072 | tf_op jit(solution)/shard_map/ppermute | solution.py:32
  10.0 1.7 %collective-permute-done = bf16[16,32]{1,0:T(8,128)(2,1)S(1)} collective-permute-done((bf16[16,32]{1,0:T(8,128)(2,1)S(1)}, bf16[16,32]{1,0:T(8,128)(2,1)S(1)}, u32[]{:S(2)}, u32[]{:S(2)}) %collective-permute-start) | collective-permute-done | bytes 1056 | tf_op jit(solution)/shard_map/ppermute | solution.py:22
  11.7 0.0 collective-permute-done.1
  11.7 0.1 concatenate.16
  11.8 1.6 %collective-permute-start.2 = (bf16[16,3648]{1,0:T(8,128)(2,1)S(1)}, bf16[16,3648]{1,0:T(8,128)(2,1)S(1)}, u32[]{:S(2)}, u32[]{:S(2)}) collective-permute-start(bf16[16,3648]{1,0:T(8,128)(2,1)S(1)} %concatenate.16), channel_id=1, source_target_pairs={{0,4},{1,5},{2,6},{3,7},{4,0},{5,1},{6,2},{7,3},{8,12},{9,13},{10,... | collective-permute-start | bytes 350216 | tf_op jit(solution)/shard_map/ppermute | solution.py:22
  13.4 0.0 collective-permute-done.5
  13.4 0.5 %collective-permute-start.9 = (bf16[16,3584]{1,0:T(8,128)(2,1)S(1)}, bf16[16,3584]{1,0:T(8,128)(2,1)S(1)}, u32[]{:S(2)}, u32[]{:S(2)}) collective-permute-start(bf16[16,3584]{1,0:T(8,128)(2,1)S(1)} %collective-permute-done.5), channel_id=1, source_target_pairs={{0,4},{1,5},{2,6},{3,7},{4,0},{5,1},{6,2},{7,3},{8,12},{9,13},{10,... | collective-permute-start | bytes 344072 | tf_op jit(solution)/shard_map/ppermute | solution.py:22
  13.8 1.5 %collective-permute-start.7 = (bf16[16,3584]{1,0:T(8,128)(2,1)S(1)}, bf16[16,3584]{1,0:T(8,128)(2,1)S(1)}, u32[]{:S(2)}, u32[]{:S(2)}) collective-permute-start(bf16[16,3584]{1,0:T(8,128)(2,1)S(1)} %collective-permute-done.5), channel_id=1, source_target_pairs={{0,2},{1,3},{2,0},{3,1},{4,6},{5,7},{6,4},{7,5},{8,10},{9,11},{10,... | collective-permute-start | bytes 344072 | tf_op jit(solution)/shard_map/ppermute | solution.py:22
  15.4 2.8 %collective-permute-done.9 = bf16[16,3584]{1,0:T(8,128)(2,1)S(1)} collective-permute-done((bf16[16,3584]{1,0:T(8,128)(2,1)S(1)}, bf16[16,3584]{1,0:T(8,128)(2,1)S(1)}, u32[]{:S(2)}, u32[]{:S(2)}) %collective-permute-start.9) | collective-permute-done | bytes 114720 | tf_op jit(solution)/shard_map/ppermute | solution.py:22
  18.2 1.5 %collective-permute-start.10 = (bf16[16,3584]{1,0:T(8,128)(2,1)S(1)}, bf16[16,3584]{1,0:T(8,128)(2,1)S(1)}, u32[]{:S(2)}, u32[]{:S(2)}) collective-permute-start(bf16[16,3584]{1,0:T(8,128)(2,1)S(1)} %collective-permute-done.9), channel_id=1, source_target_pairs={{0,2},{1,3},{2,0},{3,1},{4,6},{5,7},{6,4},{7,5},{8,10},{9,11},{10,... | collective-permute-start | bytes 344072 | tf_op jit(solution)/shard_map/ppermute | solution.py:22
  19.7 0.0 collective-permute-done.2
  19.7 0.1 concatenate.17
  19.8 0.5 %collective-permute-start.3 = (bf16[16,3712]{1,0:T(8,128)(2,1)S(1)}, bf16[16,3712]{1,0:T(8,128)(2,1)S(1)}, u32[]{:S(2)}, u32[]{:S(2)}) collective-permute-start(bf16[16,3712]{1,0:T(8,128)(2,1)S(1)} %concatenate.17), channel_id=1, source_target_pairs={{0,2},{1,3},{2,0},{3,1},{4,6},{5,7},{6,4},{7,5},{8,10},{9,11},{10,... | collective-permute-start | bytes 356360 | tf_op jit(solution)/shard_map/ppermute | solution.py:22
  20.3 0.0 collective-permute-done.6
  20.4 0.0 collective-permute-done.7
  20.4 0.1 collective-permute-start.8
  20.5 4.2 %collective-permute-done.3 = bf16[16,3712]{1,0:T(8,128)(2,1)S(1)} collective-permute-done((bf16[16,3712]{1,0:T(8,128)(2,1)S(1)}, bf16[16,3712]{1,0:T(8,128)(2,1)S(1)}, u32[]{:S(2)}, u32[]{:S(2)}) %collective-permute-start.3) | collective-permute-done | bytes 118816 | tf_op jit(solution)/shard_map/ppermute | solution.py:22
  24.7 0.0 collective-permute-done.10
  24.7 0.1 collective-permute-start.11
  24.8 0.1 pad_maximum_fusion.1.refs_4_
  24.9 0.5 %collective-permute-start.4 = (bf16[16,256]{1,0:T(8,128)(2,1)S(1)}, bf16[16,256]{1,0:T(8,128)(2,1)S(1)}, u32[]{:S(2)}, u32[]{:S(2)}) collective-permute-start(bf16[16,256]{1,0:T(8,128)(2,1)S(1)} %pad_maximum_fusion.1.refs_4_), channel_id=1, source_target_pairs={{0,1},{1,0},{2,3},{3,2},{4,5},{5,4},{6,7},{7,6},{8,9},{9,8},{10,11... | collective-permute-start | bytes 24584 | tf_op jit(solution)/shard_map/ppermute | solution.py:22
  25.4 0.1 broadcast_in_dim.6
  25.5 0.1 broadcast_in_dim_reshape.3.refs_1_
  25.5 0.9 %collective-permute-done.4.refs_5_ = bf16[16,256]{1,0:T(8,128)(2,1)S(1)} collective-permute-done((bf16[16,256]{1,0:T(8,128)(2,1)S(1)}, bf16[16,256]{1,0:T(8,128)(2,1)S(1)}, u32[]{:S(2)}, u32[]{:S(2)}) %collective-permute-start.4) | collective-permute-done | bytes 8224 | tf_op jit(solution)/shard_map/ppermute | solution.py:22
  26.5 0.0 collective-permute-done.11.refs_9_
  26.5 0.0 collective-permute-done.8.refs_7_
  26.5 6.4 %shard_map.70 = bf16[256,2048]{1,0:T(8,128)(2,1)} custom-call(s32[1]{0:T(128)} %bitcast.refs_0_, s32[1,256]{1,0:T(1,128)S(1)} %broadcast_in_dim_reshape.3.refs_1_, bf16[256,2048]{1,0:T(8,128)(2,1)} %bitcast.8, bf16[1024,3584]{1,0:T(8,128)(2,1)} %bitcast.7, bf16[16,256]{1,0:T(8,128)(2,1)S(1)} %pad_maximum_fusion.1.refs_4_, ...), custom_call_target="tpu_custom_call" | custom-call | tf_op jit(solution)/shard_map/pallas_call | solution.py:205
  (10 shorter events, 0.1 us)
Async XLA Ops:
  0.0 11.7 %collective-permute-start.1 = (bf16[16,3584]{1,0:T(8,128)(2,1)}, bf16[16,3584]{1,0:T(8,128)(2,1)S(1)}, u32[]{:S(2)}, u32[]{:S(2)}) collective-permute-start(bf16[16,3584]{1,0:T(8,128)(2,1)} %bitcast.11), channel_id=1, source_target_pairs={{0,16},{1,17},{2,18},{3,19},{4,20},{5,21},{6,22},{7,23},{8,24},{9,... | collective-permute-start | bytes 344072 | tf_op jit(solution)/shard_map/ppermute | solution.py:32
  2.9 10.4 %collective-permute-start.5 = (bf16[16,3584]{1,0:T(8,128)(2,1)}, bf16[16,3584]{1,0:T(8,128)(2,1)S(1)}, u32[]{:S(2)}, u32[]{:S(2)}) collective-permute-start(bf16[16,3584]{1,0:T(8,128)(2,1)} %bitcast.12), channel_id=1, source_target_pairs={{0,24},{1,25},{2,26},{3,27},{4,28},{5,29},{6,30},{7,31},{8,16},{9,... | collective-permute-start | bytes 344072 | tf_op jit(solution)/shard_map/ppermute | solution.py:32
  7.2 4.5 %collective-permute-start = (bf16[16,32]{1,0:T(8,128)(2,1)S(1)}, bf16[16,32]{1,0:T(8,128)(2,1)S(1)}, u32[]{:S(2)}, u32[]{:S(2)}) collective-permute-start(bf16[16,32]{1,0:T(8,128)(2,1)S(1)} %shard_map.69), channel_id=1, source_target_pairs={{0,8},{1,9},{2,10},{3,11},{4,12},{5,13},{6,14},{7,15},{8,0},{9,1},... | collective-permute-start | bytes 3080 | tf_op jit(solution)/shard_map/ppermute | solution.py:22
  7.2 13.1 %collective-permute-start.6 = (bf16[16,3584]{1,0:T(8,128)(2,1)}, bf16[16,3584]{1,0:T(8,128)(2,1)S(1)}, u32[]{:S(2)}, u32[]{:S(2)}) collective-permute-start(bf16[16,3584]{1,0:T(8,128)(2,1)} %bitcast.13), channel_id=1, source_target_pairs={{0,18},{1,19},{2,16},{3,17},{4,22},{5,23},{6,20},{7,21},{8,26},{9,... | collective-permute-start | bytes 344072 | tf_op jit(solution)/shard_map/ppermute | solution.py:32
  11.8 7.9 %collective-permute-start.2 = (bf16[16,3648]{1,0:T(8,128)(2,1)S(1)}, bf16[16,3648]{1,0:T(8,128)(2,1)S(1)}, u32[]{:S(2)}, u32[]{:S(2)}) collective-permute-start(bf16[16,3648]{1,0:T(8,128)(2,1)S(1)} %concatenate.16), channel_id=1, source_target_pairs={{0,4},{1,5},{2,6},{3,7},{4,0},{5,1},{6,2},{7,3},{8,12},{9,13},{10,... | collective-permute-start | bytes 350216 | tf_op jit(solution)/shard_map/ppermute | solution.py:22
  13.4 4.8 %collective-permute-start.9 = (bf16[16,3584]{1,0:T(8,128)(2,1)S(1)}, bf16[16,3584]{1,0:T(8,128)(2,1)S(1)}, u32[]{:S(2)}, u32[]{:S(2)}) collective-permute-start(bf16[16,3584]{1,0:T(8,128)(2,1)S(1)} %collective-permute-done.5), channel_id=1, source_target_pairs={{0,4},{1,5},{2,6},{3,7},{4,0},{5,1},{6,2},{7,3},{8,12},{9,13},{10,... | collective-permute-start | bytes 344072 | tf_op jit(solution)/shard_map/ppermute | solution.py:22
  13.8 6.5 %collective-permute-start.7 = (bf16[16,3584]{1,0:T(8,128)(2,1)S(1)}, bf16[16,3584]{1,0:T(8,128)(2,1)S(1)}, u32[]{:S(2)}, u32[]{:S(2)}) collective-permute-start(bf16[16,3584]{1,0:T(8,128)(2,1)S(1)} %collective-permute-done.5), channel_id=1, source_target_pairs={{0,2},{1,3},{2,0},{3,1},{4,6},{5,7},{6,4},{7,5},{8,10},{9,11},{10,... | collective-permute-start | bytes 344072 | tf_op jit(solution)/shard_map/ppermute | solution.py:22
  18.2 6.5 %collective-permute-start.10 = (bf16[16,3584]{1,0:T(8,128)(2,1)S(1)}, bf16[16,3584]{1,0:T(8,128)(2,1)S(1)}, u32[]{:S(2)}, u32[]{:S(2)}) collective-permute-start(bf16[16,3584]{1,0:T(8,128)(2,1)S(1)} %collective-permute-done.9), channel_id=1, source_target_pairs={{0,2},{1,3},{2,0},{3,1},{4,6},{5,7},{6,4},{7,5},{8,10},{9,11},{10,... | collective-permute-start | bytes 344072 | tf_op jit(solution)/shard_map/ppermute | solution.py:22
  19.8 4.8 %collective-permute-start.3 = (bf16[16,3712]{1,0:T(8,128)(2,1)S(1)}, bf16[16,3712]{1,0:T(8,128)(2,1)S(1)}, u32[]{:S(2)}, u32[]{:S(2)}) collective-permute-start(bf16[16,3712]{1,0:T(8,128)(2,1)S(1)} %concatenate.17), channel_id=1, source_target_pairs={{0,2},{1,3},{2,0},{3,1},{4,6},{5,7},{6,4},{7,5},{8,10},{9,11},{10,... | collective-permute-start | bytes 356360 | tf_op jit(solution)/shard_map/ppermute | solution.py:22
  20.4 6.1 %collective-permute-start.8 = (bf16[80,3584]{1,0:T(8,128)(2,1)S(1)}, bf16[80,3584]{1,0:T(8,128)(2,1)S(1)}, u32[]{:S(2)}, u32[]{:S(2)}) collective-permute-start(bf16[80,3584]{1,0:T(8,128)(2,1)S(1)} %constant_dynamic-update-slice_fusion.refs_6_), channel_id=1, source_target_pairs={{0,1},{1,0},{2,3},{3,2},{4,5},{5,4},{6,7},{7,6},{8,9},{9,8},{10,11... | collective-permute-start | bytes 1720328 | tf_op jit(solution)/shard_map/ppermute | solution.py:22
  24.7 1.7 %collective-permute-start.11 = (bf16[48,3584]{1,0:T(8,128)(2,1)S(1)}, bf16[48,3584]{1,0:T(8,128)(2,1)S(1)}, u32[]{:S(2)}, u32[]{:S(2)}) collective-permute-start(bf16[48,3584]{1,0:T(8,128)(2,1)S(1)} %pad_maximum_fusion.refs_8_), channel_id=1, source_target_pairs={{0,1},{1,0},{2,3},{3,2},{4,5},{5,4},{6,7},{7,6},{8,9},{9,8},{10,11... | collective-permute-start | bytes 1032200 | tf_op jit(solution)/shard_map/ppermute | solution.py:22
  24.9 1.6 %collective-permute-start.4 = (bf16[16,256]{1,0:T(8,128)(2,1)S(1)}, bf16[16,256]{1,0:T(8,128)(2,1)S(1)}, u32[]{:S(2)}, u32[]{:S(2)}) collective-permute-start(bf16[16,256]{1,0:T(8,128)(2,1)S(1)} %pad_maximum_fusion.1.refs_4_), channel_id=1, source_target_pairs={{0,1},{1,0},{2,3},{3,2},{4,5},{5,4},{6,7},{7,6},{8,9},{9,8},{10,11... | collective-permute-start | bytes 24584 | tf_op jit(solution)/shard_map/ppermute | solution.py:22

commit v3 on v2

v3 whole, which is shorter than its diff:
```python
import functools

import jax
import jax.numpy as jnp
from jax import lax
from jax.experimental import pallas as pl
from jax.experimental.pallas import tpu as pltpu
from jax.sharding import PartitionSpec as P

in_space = pltpu.with_memory_space_constraint

CORE = 1
PAIR = 2
ROWS = 16
W_PARTS = 4
W_LOADS = 2
FIRST_LOADS = 4
MIB = 1024 * 1024
CONTRACT_LAST = (((1,), (1,)), ((), ()))


def exchange(x, delta):
    peers = lax.axis_size("expert")
    return lax.ppermute(x, "expert", [(i, i ^ delta) for i in range(peers)])


def from_next_section(x, delta):
    sections, peers = lax.axis_size("section"), lax.axis_size("expert")
    pairs = [
        (s * peers + i, (s - 1) % sections * peers + (i ^ delta))
        for s in range(sections)
        for i in range(peers)
    ]
    return lax.ppermute(x, ("section", "expert"), pairs)


def table_kernel(routes_hbm, gates_hbm, saved_hbm, out_ref, saved_ref, routes_ref, gates_ref, sems):
    loads = [
        pltpu.make_async_copy(routes_hbm, routes_ref, sems.at[0]),
        pltpu.make_async_copy(gates_hbm, gates_ref, sems.at[1]),
        pltpu.make_async_copy(saved_hbm, saved_ref, sems.at[2]),
    ]
    for load in loads:
        load.start()
    for load in loads[:2]:
        load.wait()
    tok, experts = out_ref.shape[0], out_ref.shape[1] // 2
    ids = lax.broadcasted_iota(jnp.int32, (experts, tok), 0)
    table = jnp.zeros((experts, tok), jnp.float32)
    for k in range(routes_ref.shape[0]):
        table += jnp.where(routes_ref[k : k + 1, :] == ids, gates_ref[k : k + 1, :], 0.0)
    table = table.T
    high = table.astype(jnp.bfloat16)
    out_ref[:, :experts] = high
    out_ref[:, experts:] = (table - high.astype(jnp.float32)).astype(jnp.bfloat16)
    loads[2].wait()


def assign_table(routes, gates, saved, experts):
    vmem, hbm = pl.BlockSpec(memory_space=pltpu.VMEM), pl.BlockSpec(memory_space=pl.ANY)
    return pl.pallas_call(
        table_kernel,
        out_shape=[
            jax.ShapeDtypeStruct((routes.shape[0], 2 * experts), jnp.bfloat16),
            jax.ShapeDtypeStruct(saved.shape, saved.dtype),
        ],
        in_specs=[hbm] * 3,
        out_specs=[vmem] * 2,
        scratch_shapes=[
            pltpu.VMEM(routes.shape[::-1], routes.dtype),
            pltpu.VMEM(gates.shape[::-1], gates.dtype),
            pltpu.SemaphoreType.DMA((3,)),
        ],
        compiler_params=pltpu.CompilerParams(vmem_limit_bytes=MIB),
    )(*[in_space(x, pltpu.HBM) for x in (routes.T, gates.T, saved)])


def join_kernel(count, *refs):
    out_ref = refs[-1]
    at = 0
    for ref in refs[:count]:
        out_ref[:, at : at + ref.shape[1]] = ref[...]
        at += ref.shape[1]


def join(parts, after=()):
    vmem, hbm = pl.BlockSpec(memory_space=pltpu.VMEM), pl.BlockSpec(memory_space=pl.ANY)
    width = sum(part.shape[1] for part in parts)
    return pl.pallas_call(
        functools.partial(join_kernel, len(parts)),
        out_shape=jax.ShapeDtypeStruct((parts[0].shape[0], width), parts[0].dtype),
        in_specs=[vmem] * len(parts) + [hbm] * len(after),
        out_specs=vmem,
        compiler_params=pltpu.CompilerParams(vmem_limit_bytes=4 * MIB),
    )(*parts, *after)


def gather_tokens(grad, table):
    peers = lax.axis_size("expert")
    top = peers // 2
    middle = [1 << b for b in reversed(range(2, top.bit_length() - 1))]
    width = grad.shape[1]
    names, tables = [0], table

    def add_tables(got, delta):
        nonlocal names, tables
        names, tables = names + [k ^ delta for k in names], jnp.concatenate([tables, got], axis=1)

    def with_tables(k, delta, after=()):
        got = exchange(join([chunks[k], tables], after), delta)
        chunks[k ^ delta] = got[:, :width]
        add_tables(got[:, width:], delta)

    near, far = [0], [top]
    for delta in middle:
        near += [k ^ delta for k in near]
    chunks = {k: from_next_section(grad, k) for k in [PAIR] + near[1:] + [top, 0]}
    add_tables(exchange(tables, top), top)
    for delta in middle:
        for k in far[:-1]:
            chunks[k ^ delta] = exchange(chunks[k], delta)
        with_tables(far[-1], delta)
        far += [k ^ delta for k in far]
    rest = far + near[1:]
    for k in rest[:-1]:
        chunks[k ^ PAIR] = exchange(chunks[k], PAIR)
    with_tables(rest[-1], PAIR, after=[chunks[PAIR]])
    late = [k ^ PAIR for k in far]
    return chunks, late, [(names, tables), ([k ^ CORE for k in names], exchange(tables, CORE))]


def swap_cores(chunks, late):
    groups = []
    for part in ([k for k in chunks if k not in late], late):
        own = jnp.concatenate([chunks[k] for k in part])
        groups += [(part, own), ([k ^ CORE for k in part], exchange(own, CORE))]
    return groups


def slot_units(order, most):
    blocks = max(1, ROWS // most)
    return blocks, list(dict.fromkeys(delta // blocks for delta in order))


def slot_bases(order, most, tok, me):
    blocks, units = slot_units(order, most)
    deltas = jnp.asarray(order, jnp.int32)
    starts = jnp.asarray([units.index(delta // blocks) * blocks * most for delta in order], jnp.int32)
    return jnp.repeat(starts + (me ^ deltas) % blocks * most, tok)[None, :]


def find_slots(order, table_order, tok, me, base_ref, table_refs, table_ref):
    experts = table_ref.shape[1] // 2
    count = len(order) * tok
    for names, ref in zip(table_order, table_refs, strict=True):
        for n, k in enumerate(names):
            i = order.index(k)
            table_ref[i * tok : (i + 1) * tok, :] = ref[:, n * 2 * experts : (n + 1) * 2 * experts]
    lanes = lax.broadcasted_iota(jnp.int32, (8, 2 * experts), 1)
    pick = jnp.where((lanes == me) | (lanes == me + experts), 1.0, 0.0).astype(jnp.bfloat16)
    gate = lax.dot_general(pick, table_ref[...], CONTRACT_LAST, preferred_element_type=jnp.float32)
    live = gate > 0.0
    rows = lax.broadcasted_iota(jnp.int32, (count, count), 0)
    cols = lax.broadcasted_iota(jnp.int32, (count, count), 1)
    earlier = jnp.where((rows < cols) & (rows // tok == cols // tok), 1.0, 0.0).astype(jnp.bfloat16)
    before = lax.dot_general(
        jnp.where(live, 1.0, 0.0).astype(jnp.bfloat16),
        earlier,
        (((1,), (0,)), ((), ())),
        preferred_element_type=jnp.float32,
    )
    slot = jnp.where(live[:1], base_ref[...] + before[:1].astype(jnp.int32), -1)
    return slot, gate[:1]


def fill_rows(out_ref, token_ref, slot, gate, first, height, add=False):
    hit = first + lax.broadcasted_iota(jnp.int32, (height, slot.shape[1]), 0) == slot
    weight = jnp.sum(jnp.where(hit, gate, 0.0), axis=1, keepdims=True)
    onehot = jnp.where(hit, 1.0, 0.0).astype(jnp.bfloat16)
    width = token_ref.shape[1]
    step = 512 if width % 512 == 0 else width
    for k in range(0, width, step):
        taken = jnp.dot(onehot, token_ref[:, k : k + step], preferred_element_type=jnp.float32)
        scaled = (weight * taken).astype(out_ref.dtype)
        if add:
            scaled += out_ref[first : first + height, k : k + step]
        out_ref[first : first + height, k : k + step] = scaled


def down_kernel(order, table_order, tok, most, me_ref, base_ref, saved_ref, w_hbm, *refs):
    table_refs, token_refs = refs[: len(table_order)], refs[len(table_order) : -7]
    out_hbm, d_ref, w_ref, out_ref, table_ref, sems, out_sems = refs[-7:]
    width = w_ref.shape[0]
    blocks, units = slot_units(order, most)
    tall = blocks * most
    me = me_ref[0]
    wide = width // W_PARTS
    height = wide // W_LOADS

    def load(n):
        part = pl.ds(pl.multiple_of(n * height, height), height)
        return pltpu.make_async_copy(w_hbm.at[part], w_ref.at[part], sems.at[n])

    def stores(part):
        for half in range(2):
            span = pl.ds(pl.multiple_of(half * width + part * wide, wide), wide)
            yield pltpu.make_async_copy(out_ref.at[:, span], out_hbm.at[:, span], out_sems.at[2 * part + half])

    for n in range(FIRST_LOADS):
        load(n).start()
    slot, gate = find_slots(order, table_order, tok, me, base_ref, table_refs, table_ref)
    token, row = 0, 0
    for ref in token_refs:
        count = ref.shape[0]
        size = count // tok * most
        span = slice(token, token + count)
        if blocks == 1:
            fill_rows(d_ref, ref, slot[:, span], gate[:, span], row, size)
        else:
            fill_rows(d_ref, ref, slot[:, span], gate[:, span], 0, d_ref.shape[0], add=token > 0)
        token, row = token + count, row + size
    for n in range(FIRST_LOADS, W_PARTS * W_LOADS):
        load(n).start()

    @pl.loop(0, W_PARTS)
    def _(part):
        for n in range(W_LOADS):
            load(part * W_LOADS + n).wait()
        at = pl.multiple_of(part * wide, wide)
        hidden = lax.dot_general(
            d_ref[...], w_ref[pl.ds(at, wide), :], CONTRACT_LAST, preferred_element_type=jnp.float32
        )
        for i, delta in enumerate(units):
            place = pl.ds(pl.multiple_of((me // blocks ^ delta) * tall, tall), tall)
            h = hidden[i * tall : (i + 1) * tall]
            a = saved_ref[place, pl.ds(at, wide)].astype(jnp.float32)
            u = saved_ref[place, pl.ds(width + at, wide)].astype(jnp.float32)
            sig = jax.nn.sigmoid(a)
            hs = h * sig
            out_ref[place, pl.ds(at, wide)] = (hs * u * (1.0 + a * (1.0 - sig))).astype(out_ref.dtype)
            out_ref[place, pl.ds(width + at, wide)] = (hs * a).astype(out_ref.dtype)
        for store in stores(part):
            store.start()

    for part in range(W_PARTS):
        for store in stores(part):
            store.wait()


def per_device(next_grad, routes, gates, saved, w_down):
    experts = lax.axis_size("expert")
    slots, width = saved.shape[2:]
    most = slots // experts
    tok, features = next_grad.shape[1:]
    table, near_saved = assign_table(routes[0], gates[0], saved[0, 0], experts)
    chunks, late, tables = gather_tokens(next_grad[0], table)
    groups = swap_cores(chunks, late)
    order = [k for names, _ in groups for k in names]
    me = lax.axis_index("expert").astype(jnp.int32).reshape(1)
    smem = pl.BlockSpec(memory_space=pltpu.SMEM)
    vmem, hbm = pl.BlockSpec(memory_space=pltpu.VMEM), pl.BlockSpec(memory_space=pl.ANY)
    out = pl.pallas_call(
        functools.partial(down_kernel, order, [names for names, _ in tables], tok, most),
        out_shape=jax.ShapeDtypeStruct((slots, width), jnp.bfloat16),
        in_specs=[smem, vmem, vmem, hbm] + [vmem] * (len(tables) + len(groups)),
        out_specs=hbm,
        scratch_shapes=[
            pltpu.VMEM((slots, features), jnp.bfloat16),
            pltpu.VMEM(w_down.shape[1:], jnp.bfloat16),
            pltpu.VMEM((slots, width), jnp.bfloat16),
            pltpu.VMEM((experts * tok, 2 * experts), jnp.bfloat16),
            pltpu.SemaphoreType.DMA((W_PARTS * W_LOADS,)),
            pltpu.SemaphoreType.DMA((2 * W_PARTS,)),
        ],
        compiler_params=pltpu.CompilerParams(vmem_limit_bytes=40 * MIB),
    )(
        me,
        slot_bases(order, most, tok, me),
        near_saved,
        in_space(w_down[0], pltpu.HBM),
        *[array for _, array in tables],
        *[array for _, array in groups],
    )
    return out[None, None]


def solution(mesh):
    return jax.shard_map(
        per_device,
        mesh=mesh,
        in_specs=(
            P("section", "expert", None),
            P("section", "expert", None),
            P("section", "expert", None),
            P("section", "expert", None, None),
            P("expert", None, None),
        ),
        out_specs=P("section", "expert", None, None),
        check_vma=False,
    )
```

time: 33 us -> 31.6 us (0.958)
  local copies, waits for them, and re-layouts: 1.92 us -> 0.24 us
  waiting for transfers between devices: 9.65 us -> 8.82 us
  Pallas kernels: 6.56 us -> 7.23 us
    ppermute x9 -> x8, waiting for transfers between devices: 9.64 us -> 6.5 us  [exchange(): return lax.ppermute(x, 'expert', [(i, i ^ delta) for i in range(peers)])]
    ppermute x3 -> x4, waiting for transfers between devices: 0.01 us -> 2.32 us  [from_next_section(): return lax.ppermute(x, ('section', 'expert'), pairs)]
    squeeze x2 -> x0, local copies, waits for them, and re-layouts: 1.51 us -> none  [per_device(): table = assign_table(routes[0], gates[0], experts)]
    ppermute x3 -> x4, starting transfers between devices: 8.25 us -> 9.49 us  [from_next_section(): return lax.ppermute(x, ('section', 'expert'), pairs)]
    pallas_call x1 -> x3, Pallas kernels: 0.18 us -> 1.3 us  [the longest x1 1.28 us: assign_table(): pl.pallas_call(table_kernel, out_shape=[jax.ShapeDtypeStruct((routes.shap...]
    ppermute x9 -> x8, starting transfers between devices: 6.25 us -> 5.28 us  [exchange(): return lax.ppermute(x, 'expert', [(i, i ^ delta) for i in range(peers)])]
    pallas_call x1, Pallas kernels: 6.38 us -> 5.93 us  [per_device(): pl.pallas_call(functools.partial(down_kernel, order, [names for names, _...]
  transfers between devices with their start and end apart: 12 -> 12, of which waited for: 4 -> 8; matrix products, arithmetic and copies ran while one was open for 6% -> 2% of each run, Pallas kernels for 1% -> 4%
where the time goes in v3:
time: 31.6 us; the launch traced here: 31.4 us
  starting transfers between devices  14.8 us (47%)
  waiting for transfers between devices  8.82 us (28%)
  Pallas kernels  7.23 us (23%)
    ppermute x4, starting transfers between devices, from_next_section(): return lax.ppermute(x, ('section', 'expert'), pairs)  9.49 us
    ppermute x8, waiting for transfers between devices, exchange(): return lax.ppermute(x, 'expert', [(i, i ^ delta) for i in range(peers)])  6.5 us
    pallas_call x1, Pallas kernels, per_device(): pl.pallas_call(functools.partial(down_kernel, order, [names for names, _...  5.93 us
    ppermute x8, starting transfers between devices, exchange(): return lax.ppermute(x, 'expert', [(i, i ^ delta) for i in range(peers)])  5.28 us
    ppermute x4, waiting for transfers between devices, from_next_section(): return lax.ppermute(x, ('section', 'expert'), pairs)  2.32 us
    pallas_call x1, Pallas kernels, assign_table(): pl.pallas_call(table_kernel, out_shape=[jax.ShapeDtypeStruct((routes.shap...  1.28 us
  transfers between devices with their start and end apart: 12, of which 8 were waited for; matrix products, arithmetic and copies ran while one was open for 2% of the time, Pallas kernels for 4%

profile of v3, /device:TPU:0, one launch (start us, length us, event | category | flops | bytes accessed | tf_op | source)
XLA Modules:
  0.0 31.4 jit_solution(11475156550709146626)
XLA Ops:
  0.0 5.0 %collective-permute-start.1 = (bf16[16,3584]{1,0:T(8,128)(2,1)}, bf16[16,3584]{1,0:T(8,128)(2,1)S(1)}, u32[]{:S(2)}, u32[]{:S(2)}) collective-permute-start(bf16[16,3584]{1,0:T(8,128)(2,1)} %bitcast.15), channel_id=1, source_target_pairs={{0,24},{1,25},{2,26},{3,27},{4,28},{5,29},{6,30},{7,31},{8,16},{9,... | collective-permute-start | bytes 344072 | tf_op jit(solution)/shard_map/ppermute | solution.py:34
  5.0 1.5 %collective-permute-start.4 = (bf16[16,3584]{1,0:T(8,128)(2,1)}, bf16[16,3584]{1,0:T(8,128)(2,1)S(1)}, u32[]{:S(2)}, u32[]{:S(2)}) collective-permute-start(bf16[16,3584]{1,0:T(8,128)(2,1)} %bitcast.16), channel_id=1, source_target_pairs={{0,18},{1,19},{2,16},{3,17},{4,22},{5,23},{6,20},{7,21},{8,26},{9,... | collective-permute-start | bytes 344072 | tf_op jit(solution)/shard_map/ppermute | solution.py:34
  6.5 1.3 %shard_map.69 = (bf16[16,32]{1,0:T(8,128)(2,1)S(1)}, bf16[256,2048]{1,0:T(8,128)(2,1)S(1)}) custom-call(s32[8,16]{1,0:T(8,128)} %bitcast.13, f32[8,16]{1,0:T(8,128)} %bitcast.14, bf16[256,2048]{1,0:T(8,128)(2,1)} %bitcast.12), custom_call_target="tpu_custom_call" | custom-call | tf_op jit(solution)/shard_map/pallas_call | solution.py:61
  7.7 0.4 %collective-permute-start = (bf16[16,32]{1,0:T(8,128)(2,1)S(1)}, bf16[16,32]{1,0:T(8,128)(2,1)S(1)}, u32[]{:S(2)}, u32[]{:S(2)}) collective-permute-start(bf16[16,32]{1,0:T(8,128)(2,1)S(1)} %get-tuple-element.8), channel_id=1, source_target_pairs={{0,8},{1,9},{2,10},{3,11},{4,12},{5,13},{6,14},{7,15},{8,0},{9,1},... | collective-permute-start | bytes 3080 | tf_op jit(solution)/shard_map/ppermute | solution.py:24
  8.1 1.5 %collective-permute-start.7 = (bf16[16,3584]{1,0:T(8,128)(2,1)}, bf16[16,3584]{1,0:T(8,128)(2,1)S(1)}, u32[]{:S(2)}, u32[]{:S(2)}) collective-permute-start(bf16[16,3584]{1,0:T(8,128)(2,1)} %bitcast.17), channel_id=1, source_target_pairs={{0,16},{1,17},{2,18},{3,19},{4,20},{5,21},{6,22},{7,23},{8,24},{9,... | collective-permute-start | bytes 344072 | tf_op jit(solution)/shard_map/ppermute | solution.py:34
  9.6 1.5 %collective-permute-start.3 = (bf16[16,3584]{1,0:T(8,128)(2,1)}, bf16[16,3584]{1,0:T(8,128)(2,1)S(1)}, u32[]{:S(2)}, u32[]{:S(2)}) collective-permute-start(bf16[16,3584]{1,0:T(8,128)(2,1)} %bitcast.18), channel_id=1, source_target_pairs={{0,20},{1,21},{2,22},{3,23},{4,16},{5,17},{6,18},{7,19},{8,28},{9,... | collective-permute-start | bytes 344072 | tf_op jit(solution)/shard_map/ppermute | solution.py:34
  11.2 1.2 %collective-permute-done = bf16[16,32]{1,0:T(8,128)(2,1)S(1)} collective-permute-done((bf16[16,32]{1,0:T(8,128)(2,1)S(1)}, bf16[16,32]{1,0:T(8,128)(2,1)S(1)}, u32[]{:S(2)}, u32[]{:S(2)}) %collective-permute-start) | collective-permute-done | bytes 1056 | tf_op jit(solution)/shard_map/ppermute | solution.py:24
  12.4 0.1 pad_maximum_fusion.1.refs_1_
  12.5 0.0 collective-permute-done.1.refs_0_
  12.5 1.6 %collective-permute-start.2 = (bf16[16,3648]{1,0:T(8,128)(2,1)S(1)}, bf16[16,3648]{1,0:T(8,128)(2,1)S(1)}, u32[]{:S(2)}, u32[]{:S(2)}) collective-permute-start(bf16[16,3648]{1,0:T(8,128)(2,1)S(1)} %shard_map.70), channel_id=1, source_target_pairs={{0,4},{1,5},{2,6},{3,7},{4,0},{5,1},{6,2},{7,3},{8,12},{9,13},{10,... | collective-permute-start | bytes 350216 | tf_op jit(solution)/shard_map/ppermute | solution.py:24
  14.1 0.5 %collective-permute-start.9 = (bf16[16,3584]{1,0:T(8,128)(2,1)S(1)}, bf16[16,3584]{1,0:T(8,128)(2,1)S(1)}, u32[]{:S(2)}, u32[]{:S(2)}) collective-permute-start(bf16[16,3584]{1,0:T(8,128)(2,1)S(1)} %collective-permute-done.1.refs_0_), channel_id=1, source_target_pairs={{0,2},{1,3},{2,0},{3,1},{4,6},{5,7},{6,4},{7,5},{8,10},{9,11},{10,... | collective-permute-start | bytes 344072 | tf_op jit(solution)/shard_map/ppermute | solution.py:24
  14.6 0.1 collective-permute-done.4.refs_2_
  14.8 1.9 %collective-permute-done.3.refs_0_ = bf16[16,3584]{1,0:T(8,128)(2,1)S(1)} collective-permute-done((bf16[16,3584]{1,0:T(8,128)(2,1)}, bf16[16,3584]{1,0:T(8,128)(2,1)S(1)}, u32[]{:S(2)}, u32[]{:S(2)}) %collective-permute-start.3) | collective-permute-done | bytes 114720 | tf_op jit(solution)/shard_map/ppermute | solution.py:34
  16.7 0.3 collective-permute-done.7
  17.0 0.4 %collective-permute-done.2 = bf16[16,3648]{1,0:T(8,128)(2,1)S(1)} collective-permute-done((bf16[16,3648]{1,0:T(8,128)(2,1)S(1)}, bf16[16,3648]{1,0:T(8,128)(2,1)S(1)}, u32[]{:S(2)}, u32[]{:S(2)}) %collective-permute-start.2) | collective-permute-done | bytes 116768 | tf_op jit(solution)/shard_map/ppermute | solution.py:24
  17.4 0.1 pad_maximum_fusion.2.refs_1_
  17.5 0.5 %collective-permute-start.5 = (bf16[16,3712]{1,0:T(8,128)(2,1)S(1)}, bf16[16,3712]{1,0:T(8,128)(2,1)S(1)}, u32[]{:S(2)}, u32[]{:S(2)}) collective-permute-start(bf16[16,3712]{1,0:T(8,128)(2,1)S(1)} %shard_map.71), channel_id=1, source_target_pairs={{0,2},{1,3},{2,0},{3,1},{4,6},{5,7},{6,4},{7,5},{8,10},{9,11},{10,... | collective-permute-start | bytes 356360 | tf_op jit(solution)/shard_map/ppermute | solution.py:24
  18.0 1.7 %collective-permute-start.10 = (bf16[16,3584]{1,0:T(8,128)(2,1)S(1)}, bf16[16,3584]{1,0:T(8,128)(2,1)S(1)}, u32[]{:S(2)}, u32[]{:S(2)}) collective-permute-start(bf16[16,3584]{1,0:T(8,128)(2,1)S(1)} %get-tuple-element.9), channel_id=1, source_target_pairs={{0,2},{1,3},{2,0},{3,1},{4,6},{5,7},{6,4},{7,5},{8,10},{9,11},{10,... | collective-permute-start | bytes 344072 | tf_op jit(solution)/shard_map/ppermute | solution.py:24
  19.7 3.0 %collective-permute-done.5 = bf16[16,3712]{1,0:T(8,128)(2,1)S(1)} collective-permute-done((bf16[16,3712]{1,0:T(8,128)(2,1)S(1)}, bf16[16,3712]{1,0:T(8,128)(2,1)S(1)}, u32[]{:S(2)}, u32[]{:S(2)}) %collective-permute-start.5) | collective-permute-done | bytes 118816 | tf_op jit(solution)/shard_map/ppermute | solution.py:24
  22.7 0.1 collective-permute-start.8
  22.8 0.0 collective-permute-done.9
  22.8 1.1 %collective-permute-done.10 = bf16[16,3584]{1,0:T(8,128)(2,1)S(1)} collective-permute-done((bf16[16,3584]{1,0:T(8,128)(2,1)S(1)}, bf16[16,3584]{1,0:T(8,128)(2,1)S(1)}, u32[]{:S(2)}, u32[]{:S(2)}) %collective-permute-start.10) | collective-permute-done | bytes 114720 | tf_op jit(solution)/shard_map/ppermute | solution.py:24
  23.9 0.1 collective-permute-start.11
  24.0 0.1 pad_maximum_fusion.refs_0_
  24.1 0.5 %collective-permute-start.6 = (bf16[16,256]{1,0:T(8,128)(2,1)S(1)}, bf16[16,256]{1,0:T(8,128)(2,1)S(1)}, u32[]{:S(2)}, u32[]{:S(2)}) collective-permute-start(bf16[16,256]{1,0:T(8,128)(2,1)S(1)} %pad_maximum_fusion.refs_0_), channel_id=1, source_target_pairs={{0,1},{1,0},{2,3},{3,2},{4,5},{5,4},{6,7},{7,6},{8,9},{9,8},{10,11... | collective-permute-start | bytes 24584 | tf_op jit(solution)/shard_map/ppermute | solution.py:24
  24.6 0.1 broadcast_in_dim.6
  24.6 0.1 broadcast_in_dim_reshape.3.base_ref
  24.7 0.7 %collective-permute-done.6.refs_1_ = bf16[16,256]{1,0:T(8,128)(2,1)S(1)} collective-permute-done((bf16[16,256]{1,0:T(8,128)(2,1)S(1)}, bf16[16,256]{1,0:T(8,128)(2,1)S(1)}, u32[]{:S(2)}, u32[]{:S(2)}) %collective-permute-start.6) | collective-permute-done | bytes 8224 | tf_op jit(solution)/shard_map/ppermute | solution.py:24
  25.5 0.0 collective-permute-done.11.refs_5_
  25.5 0.0 collective-permute-done.8.refs_3_
  25.5 5.9 %shard_map.72 = bf16[256,2048]{1,0:T(8,128)(2,1)} custom-call(s32[1]{0:T(128)} %bitcast.me_ref, s32[1,256]{1,0:T(1,128)S(1)} %broadcast_in_dim_reshape.3.base_ref, bf16[256,2048]{1,0:T(8,128)(2,1)S(1)} %get-tuple-element.7.saved_ref, bf16[1024,3584]{1,0:T(8,128)(2,1)} %bitcast.11, bf16[16,256]{1,0:T(8,128)(2,1)S(1)} %pad_maximum_fusion.refs_0_, ...), custom_call_target="tpu_custom_call" | custom-call | tf_op jit(solution)/shard_map/pallas_call | solution.py:262
  (13 shorter events, 0.1 us)
Async XLA Ops:
  0.0 12.5 %collective-permute-start.1 = (bf16[16,3584]{1,0:T(8,128)(2,1)}, bf16[16,3584]{1,0:T(8,128)(2,1)S(1)}, u32[]{:S(2)}, u32[]{:S(2)}) collective-permute-start(bf16[16,3584]{1,0:T(8,128)(2,1)} %bitcast.15), channel_id=1, source_target_pairs={{0,24},{1,25},{2,26},{3,27},{4,28},{5,29},{6,30},{7,31},{8,16},{9,... | collective-permute-start | bytes 344072 | tf_op jit(solution)/shard_map/ppermute | solution.py:34
  5.0 9.8 %collective-permute-start.4 = (bf16[16,3584]{1,0:T(8,128)(2,1)}, bf16[16,3584]{1,0:T(8,128)(2,1)S(1)}, u32[]{:S(2)}, u32[]{:S(2)}) collective-permute-start(bf16[16,3584]{1,0:T(8,128)(2,1)} %bitcast.16), channel_id=1, source_target_pairs={{0,18},{1,19},{2,16},{3,17},{4,22},{5,23},{6,20},{7,21},{8,26},{9,... | collective-permute-start | bytes 344072 | tf_op jit(solution)/shard_map/ppermute | solution.py:34
  7.7 4.7 %collective-permute-start = (bf16[16,32]{1,0:T(8,128)(2,1)S(1)}, bf16[16,32]{1,0:T(8,128)(2,1)S(1)}, u32[]{:S(2)}, u32[]{:S(2)}) collective-permute-start(bf16[16,32]{1,0:T(8,128)(2,1)S(1)} %get-tuple-element.8), channel_id=1, source_target_pairs={{0,8},{1,9},{2,10},{3,11},{4,12},{5,13},{6,14},{7,15},{8,0},{9,1},... | collective-permute-start | bytes 3080 | tf_op jit(solution)/shard_map/ppermute | solution.py:24
  8.1 8.8 %collective-permute-start.7 = (bf16[16,3584]{1,0:T(8,128)(2,1)}, bf16[16,3584]{1,0:T(8,128)(2,1)S(1)}, u32[]{:S(2)}, u32[]{:S(2)}) collective-permute-start(bf16[16,3584]{1,0:T(8,128)(2,1)} %bitcast.17), channel_id=1, source_target_pairs={{0,16},{1,17},{2,18},{3,19},{4,20},{5,21},{6,22},{7,23},{8,24},{9,... | collective-permute-start | bytes 344072 | tf_op jit(solution)/shard_map/ppermute | solution.py:34
  9.6 7.0 %collective-permute-start.3 = (bf16[16,3584]{1,0:T(8,128)(2,1)}, bf16[16,3584]{1,0:T(8,128)(2,1)S(1)}, u32[]{:S(2)}, u32[]{:S(2)}) collective-permute-start(bf16[16,3584]{1,0:T(8,128)(2,1)} %bitcast.18), channel_id=1, source_target_pairs={{0,20},{1,21},{2,22},{3,23},{4,16},{5,17},{6,18},{7,19},{8,28},{9,... | collective-permute-start | bytes 344072 | tf_op jit(solution)/shard_map/ppermute | solution.py:34
  12.5 4.9 %collective-permute-start.2 = (bf16[16,3648]{1,0:T(8,128)(2,1)S(1)}, bf16[16,3648]{1,0:T(8,128)(2,1)S(1)}, u32[]{:S(2)}, u32[]{:S(2)}) collective-permute-start(bf16[16,3648]{1,0:T(8,128)(2,1)S(1)} %shard_map.70), channel_id=1, source_target_pairs={{0,4},{1,5},{2,6},{3,7},{4,0},{5,1},{6,2},{7,3},{8,12},{9,13},{10,... | collective-permute-start | bytes 350216 | tf_op jit(solution)/shard_map/ppermute | solution.py:24
  14.1 8.7 %collective-permute-start.9 = (bf16[16,3584]{1,0:T(8,128)(2,1)S(1)}, bf16[16,3584]{1,0:T(8,128)(2,1)S(1)}, u32[]{:S(2)}, u32[]{:S(2)}) collective-permute-start(bf16[16,3584]{1,0:T(8,128)(2,1)S(1)} %collective-permute-done.1.refs_0_), channel_id=1, source_target_pairs={{0,2},{1,3},{2,0},{3,1},{4,6},{5,7},{6,4},{7,5},{8,10},{9,11},{10,... | collective-permute-start | bytes 344072 | tf_op jit(solution)/shard_map/ppermute | solution.py:24
  17.5 5.2 %collective-permute-start.5 = (bf16[16,3712]{1,0:T(8,128)(2,1)S(1)}, bf16[16,3712]{1,0:T(8,128)(2,1)S(1)}, u32[]{:S(2)}, u32[]{:S(2)}) collective-permute-start(bf16[16,3712]{1,0:T(8,128)(2,1)S(1)} %shard_map.71), channel_id=1, source_target_pairs={{0,2},{1,3},{2,0},{3,1},{4,6},{5,7},{6,4},{7,5},{8,10},{9,11},{10,... | collective-permute-start | bytes 356360 | tf_op jit(solution)/shard_map/ppermute | solution.py:24
  18.0 5.9 %collective-permute-start.10 = (bf16[16,3584]{1,0:T(8,128)(2,1)S(1)}, bf16[16,3584]{1,0:T(8,128)(2,1)S(1)}, u32[]{:S(2)}, u32[]{:S(2)}) collective-permute-start(bf16[16,3584]{1,0:T(8,128)(2,1)S(1)} %get-tuple-element.9), channel_id=1, source_target_pairs={{0,2},{1,3},{2,0},{3,1},{4,6},{5,7},{6,4},{7,5},{8,10},{9,11},{10,... | collective-permute-start | bytes 344072 | tf_op jit(solution)/shard_map/ppermute | solution.py:24
  22.7 2.8 %collective-permute-start.8 = (bf16[96,3584]{1,0:T(8,128)(2,1)S(1)}, bf16[96,3584]{1,0:T(8,128)(2,1)S(1)}, u32[]{:S(2)}, u32[]{:S(2)}) collective-permute-start(bf16[96,3584]{1,0:T(8,128)(2,1)S(1)} %slice_dynamic-update-slice_fusion.refs_2_), channel_id=1, source_target_pairs={{0,1},{1,0},{2,3},{3,2},{4,5},{5,4},{6,7},{7,6},{8,9},{9,8},{10,11... | collective-permute-start | bytes 2064392 | tf_op jit(solution)/shard_map/ppermute | solution.py:24
  23.9 1.6 %collective-permute-start.11 = (bf16[32,3584]{1,0:T(8,128)(2,1)S(1)}, bf16[32,3584]{1,0:T(8,128)(2,1)S(1)}, u32[]{:S(2)}, u32[]{:S(2)}) collective-permute-start(bf16[32,3584]{1,0:T(8,128)(2,1)S(1)} %constant_dynamic-update-slice_fusion.5.refs_4_), channel_id=1, source_target_pairs={{0,1},{1,0},{2,3},{3,2},{4,5},{5,4},{6,7},{7,6},{8,9},{9,8},{10,11... | collective-permute-start | bytes 688136 | tf_op jit(solution)/shard_map/ppermute | solution.py:24
  24.1 1.4 %collective-permute-start.6 = (bf16[16,256]{1,0:T(8,128)(2,1)S(1)}, bf16[16,256]{1,0:T(8,128)(2,1)S(1)}, u32[]{:S(2)}, u32[]{:S(2)}) collective-permute-start(bf16[16,256]{1,0:T(8,128)(2,1)S(1)} %pad_maximum_fusion.refs_0_), channel_id=1, source_target_pairs={{0,1},{1,0},{2,3},{3,2},{4,5},{5,4},{6,7},{7,6},{8,9},{9,8},{10,11... | collective-permute-start | bytes 24584 | tf_op jit(solution)/shard_map/ppermute | solution.py:24

commit v4 on v3

--- a/solution.py
+++ b/solution.py
@@ -14,7 +14,6 @@
 ROWS = 16
 W_PARTS = 4
 W_LOADS = 2
-FIRST_LOADS = 4
 MIB = 1024 * 1024
 CONTRACT_LAST = (((1,), (1,)), ((), ()))
 
@@ -125,20 +124,23 @@
     for k in rest[:-1]:
         chunks[k ^ PAIR] = exchange(chunks[k], PAIR)
     with_tables(rest[-1], PAIR, after=[chunks[PAIR]])
-    late = [k ^ PAIR for k in far]
+    late = [near[-1] ^ PAIR, far[-1] ^ PAIR]
     return chunks, late, [(names, tables), ([k ^ CORE for k in names], exchange(tables, CORE))]
 
 
-def swap_cores(chunks, late):
+def swap_cores(chunks, late, waits):
+    early = [k for k in chunks if k not in late]
     groups = []
-    for part in ([k for k in chunks if k not in late], late):
+    for part, after in ((early, ()), (late, waits)):
         own = jnp.concatenate([chunks[k] for k in part])
-        groups += [(part, own), ([k ^ CORE for k in part], exchange(own, CORE))]
+        if after:
+            own = join([own], after=after)
+        groups.append([(part, own), ([k ^ CORE for k in part], exchange(own, CORE))])
     return groups
 
 
 def slot_units(order, most):
-    blocks = max(1, ROWS // most)
+    blocks = -(-ROWS // most)
     return blocks, list(dict.fromkeys(delta // blocks for delta in order))
 
 
@@ -187,9 +189,28 @@
         out_ref[first : first + height, k : k + step] = scaled
 
 
-def down_kernel(order, table_order, tok, most, me_ref, base_ref, saved_ref, w_hbm, *refs):
-    table_refs, token_refs = refs[: len(table_order)], refs[len(table_order) : -7]
-    out_hbm, d_ref, w_ref, out_ref, table_ref, sems, out_sems = refs[-7:]
+def arrange_kernel(order, table_order, tok, most, *refs):
+    me_ref, base_ref = refs[:2]
+    table_refs = refs[2 : 2 + len(table_order)]
+    token_refs = refs[2 + len(table_order) : -4]
+    rows_ref, slot_ref, gate_ref, table_ref = refs[-4:]
+    slot, gate = find_slots(order, table_order, tok, me_ref[0], base_ref, table_refs, table_ref)
+    slot_ref[...] = slot
+    gate_ref[...] = gate
+    token, row = 0, 0
+    for ref in token_refs:
+        count = ref.shape[0]
+        height = count // tok * most
+        span = slice(token, token + count)
+        if rows_ref.shape[0] < base_ref.shape[1] // tok * most:
+            fill_rows(rows_ref, ref, slot[:, span], gate[:, span], row, height)
+        else:
+            fill_rows(rows_ref, ref, slot[:, span], gate[:, span], 0, rows_ref.shape[0], add=token > 0)
+        token, row = token + count, row + height
+
+
+def down_kernel(order, tok, most, me_ref, slot_ref, gate_ref, saved_ref, w_hbm, early_ref, *refs):
+    token_refs, (out_hbm, d_ref, w_ref, out_ref, sems, out_sems) = refs[:-6], refs[-6:]
     width = w_ref.shape[0]
     blocks, units = slot_units(order, most)
     tall = blocks * most
@@ -206,21 +227,20 @@
             span = pl.ds(pl.multiple_of(half * width + part * wide, wide), wide)
             yield pltpu.make_async_copy(out_ref.at[:, span], out_hbm.at[:, span], out_sems.at[2 * part + half])
 
-    for n in range(FIRST_LOADS):
+    for n in range(W_PARTS * W_LOADS):
         load(n).start()
-    slot, gate = find_slots(order, table_order, tok, me, base_ref, table_refs, table_ref)
-    token, row = 0, 0
+    row = early_ref.shape[0]
+    d_ref[:row, :] = early_ref[...]
+    token = len(order) * tok - sum(ref.shape[0] for ref in token_refs)
     for ref in token_refs:
         count = ref.shape[0]
         size = count // tok * most
         span = slice(token, token + count)
         if blocks == 1:
-            fill_rows(d_ref, ref, slot[:, span], gate[:, span], row, size)
+            fill_rows(d_ref, ref, slot_ref[:, span], gate_ref[:, span], row, size)
         else:
-            fill_rows(d_ref, ref, slot[:, span], gate[:, span], 0, d_ref.shape[0], add=token > 0)
+            fill_rows(d_ref, ref, slot_ref[:, span], gate_ref[:, span], 0, d_ref.shape[0], add=True)
         token, row = token + count, row + size
-    for n in range(FIRST_LOADS, W_PARTS * W_LOADS):
-        load(n).start()
 
     @pl.loop(0, W_PARTS)
     def _(part):
@@ -254,32 +274,54 @@
     tok, features = next_grad.shape[1:]
     table, near_saved = assign_table(routes[0], gates[0], saved[0, 0], experts)
     chunks, late, tables = gather_tokens(next_grad[0], table)
-    groups = swap_cores(chunks, late)
-    order = [k for names, _ in groups for k in names]
+    pairs = swap_cores(chunks, late, [array for _, array in tables[1:]])
+    (early_own, early_other), (late_own, late_other) = pairs
+    order = [k for names, _ in (early_own, early_other, late_own, late_other) for k in names]
     me = lax.axis_index("expert").astype(jnp.int32).reshape(1)
     smem = pl.BlockSpec(memory_space=pltpu.SMEM)
     vmem, hbm = pl.BlockSpec(memory_space=pltpu.VMEM), pl.BlockSpec(memory_space=pl.ANY)
+    count = experts * tok
+    early = early_own[1].shape[0] * 2 // tok * most if most >= ROWS else slots
+    rows, slot, gate = pl.pallas_call(
+        functools.partial(arrange_kernel, order, [names for names, _ in tables], tok, most),
+        out_shape=[
+            jax.ShapeDtypeStruct((early, features), jnp.bfloat16),
+            jax.ShapeDtypeStruct((1, count), jnp.int32),
+            jax.ShapeDtypeStruct((1, count), jnp.float32),
+        ],
+        in_specs=[smem] + [vmem] * (1 + len(tables) + 2),
+        out_specs=[vmem] * 3,
+        scratch_shapes=[pltpu.VMEM((count, 2 * experts), jnp.bfloat16)],
+        compiler_params=pltpu.CompilerParams(vmem_limit_bytes=16 * MIB),
+    )(
+        me,
+        slot_bases(order, most, tok, me),
+        *[array for _, array in tables],
+        early_own[1],
+        early_other[1],
+    )
     out = pl.pallas_call(
-        functools.partial(down_kernel, order, [names for names, _ in tables], tok, most),
+        functools.partial(down_kernel, order, tok, most),
         out_shape=jax.ShapeDtypeStruct((slots, width), jnp.bfloat16),
-        in_specs=[smem, vmem, vmem, hbm] + [vmem] * (len(tables) + len(groups)),
+        in_specs=[smem, vmem, vmem, vmem, hbm, vmem, vmem, vmem],
         out_specs=hbm,
         scratch_shapes=[
             pltpu.VMEM((slots, features), jnp.bfloat16),
             pltpu.VMEM(w_down.shape[1:], jnp.bfloat16),
             pltpu.VMEM((slots, width), jnp.bfloat16),
-            pltpu.VMEM((experts * tok, 2 * experts), jnp.bfloat16),
             pltpu.SemaphoreType.DMA((W_PARTS * W_LOADS,)),
             pltpu.SemaphoreType.DMA((2 * W_PARTS,)),
         ],
         compiler_params=pltpu.CompilerParams(vmem_limit_bytes=40 * MIB),
     )(
         me,
-        slot_bases(order, most, tok, me),
+        slot,
+        gate,
         near_saved,
         in_space(w_down[0], pltpu.HBM),
-        *[array for _, array in tables],
-        *[array for _, array in groups],
+        rows,
+        late_own[1],
+        late_other[1],
     )
     return out[None, None]
 

time: 31.6 us -> 30.9 us (0.978)
  waiting for transfers between devices: 8.82 us -> 8.18 us
    ppermute x8, waiting for transfers between devices: 6.5 us -> 5.82 us  [exchange(): return lax.ppermute(x, 'expert', [(i, i ^ delta) for i in range(peers)])]
    pallas_call x1 -> x2, Pallas kernels: 5.93 us -> 6.1 us  [the longest x1 5.24 us: per_device(): pl.pallas_call(functools.partial(down_kernel, order, tok, most), out_shap...]
  transfers between devices with their start and end apart: 12 -> 12, of which waited for: 8 -> 7; matrix products, arithmetic and copies ran while one was open for 2% -> 2% of each run, Pallas kernels for 4% -> 7%
where the time goes in v4:
time: 30.9 us; the launch traced here: 30.7 us
  starting transfers between devices  14.5 us (47%)
  waiting for transfers between devices  8.18 us (26%)
  Pallas kernels  7.42 us (24%)
    ppermute x4, starting transfers between devices, from_next_section(): return lax.ppermute(x, ('section', 'expert'), pairs)  9.49 us
    ppermute x8, waiting for transfers between devices, exchange(): return lax.ppermute(x, 'expert', [(i, i ^ delta) for i in range(peers)])  5.82 us
    pallas_call x1, Pallas kernels, per_device(): pl.pallas_call(functools.partial(down_kernel, order, tok, most), out_shap...  5.24 us
    ppermute x8, starting transfers between devices, exchange(): return lax.ppermute(x, 'expert', [(i, i ^ delta) for i in range(peers)])  5.01 us
    ppermute x4, waiting for transfers between devices, from_next_section(): return lax.ppermute(x, ('section', 'expert'), pairs)  2.35 us
    pallas_call x1, Pallas kernels, assign_table(): pl.pallas_call(table_kernel, out_shape=[jax.ShapeDtypeStruct((routes.shap...  1.28 us
    pallas_call x1, Pallas kernels, per_device(): pl.pallas_call(functools.partial(arrange_kernel, order, [names for names,...  0.86 us
  transfers between devices with their start and end apart: 12, of which 7 were waited for; matrix products, arithmetic and copies ran while one was open for 2% of the time, Pallas kernels for 7%

profile of v4, /device:TPU:0, one launch (start us, length us, event | category | flops | bytes accessed | tf_op | source)
XLA Modules:
  0.0 30.7 jit_solution(1967648038037176473)
XLA Ops:
  0.0 5.0 %collective-permute-start.1 = (bf16[16,3584]{1,0:T(8,128)(2,1)}, bf16[16,3584]{1,0:T(8,128)(2,1)S(1)}, u32[]{:S(2)}, u32[]{:S(2)}) collective-permute-start(bf16[16,3584]{1,0:T(8,128)(2,1)} %bitcast.15), channel_id=1, source_target_pairs={{0,24},{1,25},{2,26},{3,27},{4,28},{5,29},{6,30},{7,31},{8,16},{9,... | collective-permute-start | bytes 344072 | tf_op jit(solution)/shard_map/ppermute | solution.py:33
  5.0 1.5 %collective-permute-start.4 = (bf16[16,3584]{1,0:T(8,128)(2,1)}, bf16[16,3584]{1,0:T(8,128)(2,1)S(1)}, u32[]{:S(2)}, u32[]{:S(2)}) collective-permute-start(bf16[16,3584]{1,0:T(8,128)(2,1)} %bitcast.16), channel_id=1, source_target_pairs={{0,18},{1,19},{2,16},{3,17},{4,22},{5,23},{6,20},{7,21},{8,26},{9,... | collective-permute-start | bytes 344072 | tf_op jit(solution)/shard_map/ppermute | solution.py:33
  6.5 1.3 %shard_map.69 = (bf16[16,32]{1,0:T(8,128)(2,1)S(1)}, bf16[256,2048]{1,0:T(8,128)(2,1)S(1)}) custom-call(s32[8,16]{1,0:T(8,128)} %bitcast.13, f32[8,16]{1,0:T(8,128)} %bitcast.14, bf16[256,2048]{1,0:T(8,128)(2,1)} %bitcast.12), custom_call_target="tpu_custom_call" | custom-call | tf_op jit(solution)/shard_map/pallas_call | solution.py:60
  7.7 0.4 %collective-permute-start = (bf16[16,32]{1,0:T(8,128)(2,1)S(1)}, bf16[16,32]{1,0:T(8,128)(2,1)S(1)}, u32[]{:S(2)}, u32[]{:S(2)}) collective-permute-start(bf16[16,32]{1,0:T(8,128)(2,1)S(1)} %get-tuple-element.10), channel_id=1, source_target_pairs={{0,8},{1,9},{2,10},{3,11},{4,12},{5,13},{6,14},{7,15},{8,0},{9,1},... | collective-permute-start | bytes 3080 | tf_op jit(solution)/shard_map/ppermute | solution.py:23
  8.1 2.5 %collective-permute-start.3 = (bf16[16,3584]{1,0:T(8,128)(2,1)}, bf16[16,3584]{1,0:T(8,128)(2,1)S(1)}, u32[]{:S(2)}, u32[]{:S(2)}) collective-permute-start(bf16[16,3584]{1,0:T(8,128)(2,1)} %bitcast.17), channel_id=1, source_target_pairs={{0,20},{1,21},{2,22},{3,23},{4,16},{5,17},{6,18},{7,19},{8,28},{9,... | collective-permute-start | bytes 344072 | tf_op jit(solution)/shard_map/ppermute | solution.py:33
  10.7 0.5 %collective-permute-start.7 = (bf16[16,3584]{1,0:T(8,128)(2,1)}, bf16[16,3584]{1,0:T(8,128)(2,1)S(1)}, u32[]{:S(2)}, u32[]{:S(2)}) collective-permute-start(bf16[16,3584]{1,0:T(8,128)(2,1)} %bitcast.18), channel_id=1, source_target_pairs={{0,16},{1,17},{2,18},{3,19},{4,20},{5,21},{6,22},{7,23},{8,24},{9,... | collective-permute-start | bytes 344072 | tf_op jit(solution)/shard_map/ppermute | solution.py:33
  11.2 1.1 %collective-permute-done = bf16[16,32]{1,0:T(8,128)(2,1)S(1)} collective-permute-done((bf16[16,32]{1,0:T(8,128)(2,1)S(1)}, bf16[16,32]{1,0:T(8,128)(2,1)S(1)}, u32[]{:S(2)}, u32[]{:S(2)}) %collective-permute-start) | collective-permute-done | bytes 1056 | tf_op jit(solution)/shard_map/ppermute | solution.py:23
  12.3 0.1 pad_maximum_fusion.2.refs_1_
  12.4 0.0 collective-permute-done.1.refs_0_
  12.4 1.6 %collective-permute-start.2 = (bf16[16,3648]{1,0:T(8,128)(2,1)S(1)}, bf16[16,3648]{1,0:T(8,128)(2,1)S(1)}, u32[]{:S(2)}, u32[]{:S(2)}) collective-permute-start(bf16[16,3648]{1,0:T(8,128)(2,1)S(1)} %shard_map.70), channel_id=1, source_target_pairs={{0,4},{1,5},{2,6},{3,7},{4,0},{5,1},{6,2},{7,3},{8,12},{9,13},{10,... | collective-permute-start | bytes 350216 | tf_op jit(solution)/shard_map/ppermute | solution.py:23
  14.1 0.5 %collective-permute-start.8 = (bf16[16,3584]{1,0:T(8,128)(2,1)S(1)}, bf16[16,3584]{1,0:T(8,128)(2,1)S(1)}, u32[]{:S(2)}, u32[]{:S(2)}) collective-permute-start(bf16[16,3584]{1,0:T(8,128)(2,1)S(1)} %collective-permute-done.1.refs_0_), channel_id=1, source_target_pairs={{0,2},{1,3},{2,0},{3,1},{4,6},{5,7},{6,4},{7,5},{8,10},{9,11},{10,... | collective-permute-start | bytes 344072 | tf_op jit(solution)/shard_map/ppermute | solution.py:23
  14.6 0.4 %collective-permute-done.4.refs_2_ = bf16[16,3584]{1,0:T(8,128)(2,1)S(1)} collective-permute-done((bf16[16,3584]{1,0:T(8,128)(2,1)}, bf16[16,3584]{1,0:T(8,128)(2,1)S(1)}, u32[]{:S(2)}, u32[]{:S(2)}) %collective-permute-start.4) | collective-permute-done | bytes 114720 | tf_op jit(solution)/shard_map/ppermute | solution.py:33
  15.0 0.0 collective-permute-done.3.refs_0_
  15.0 2.0 %collective-permute-done.7 = bf16[16,3584]{1,0:T(8,128)(2,1)S(1)} collective-permute-done((bf16[16,3584]{1,0:T(8,128)(2,1)}, bf16[16,3584]{1,0:T(8,128)(2,1)S(1)}, u32[]{:S(2)}, u32[]{:S(2)}) %collective-permute-start.7) | collective-permute-done | bytes 114720 | tf_op jit(solution)/shard_map/ppermute | solution.py:33
  17.0 0.3 %collective-permute-done.2 = bf16[16,3648]{1,0:T(8,128)(2,1)S(1)} collective-permute-done((bf16[16,3648]{1,0:T(8,128)(2,1)S(1)}, bf16[16,3648]{1,0:T(8,128)(2,1)S(1)}, u32[]{:S(2)}, u32[]{:S(2)}) %collective-permute-start.2) | collective-permute-done | bytes 116768 | tf_op jit(solution)/shard_map/ppermute | solution.py:23
  17.3 0.1 pad_maximum_fusion.3.refs_1_
  17.4 0.6 %collective-permute-start.5 = (bf16[16,3712]{1,0:T(8,128)(2,1)S(1)}, bf16[16,3712]{1,0:T(8,128)(2,1)S(1)}, u32[]{:S(2)}, u32[]{:S(2)}) collective-permute-start(bf16[16,3712]{1,0:T(8,128)(2,1)S(1)} %shard_map.71), channel_id=1, source_target_pairs={{0,2},{1,3},{2,0},{3,1},{4,6},{5,7},{6,4},{7,5},{8,10},{9,11},{10,... | collective-permute-start | bytes 356360 | tf_op jit(solution)/shard_map/ppermute | solution.py:23
  18.0 1.6 %collective-permute-start.10 = (bf16[16,3584]{1,0:T(8,128)(2,1)S(1)}, bf16[16,3584]{1,0:T(8,128)(2,1)S(1)}, u32[]{:S(2)}, u32[]{:S(2)}) collective-permute-start(bf16[16,3584]{1,0:T(8,128)(2,1)S(1)} %get-tuple-element.15), channel_id=1, source_target_pairs={{0,2},{1,3},{2,0},{3,1},{4,6},{5,7},{6,4},{7,5},{8,10},{9,11},{10,... | collective-permute-start | bytes 344072 | tf_op jit(solution)/shard_map/ppermute | solution.py:23
  19.6 0.0 collective-permute-done.8
  19.6 0.1 collective-permute-start.9
  19.7 2.9 %collective-permute-done.5 = bf16[16,3712]{1,0:T(8,128)(2,1)S(1)} collective-permute-done((bf16[16,3712]{1,0:T(8,128)(2,1)S(1)}, bf16[16,3712]{1,0:T(8,128)(2,1)S(1)}, u32[]{:S(2)}, u32[]{:S(2)}) %collective-permute-start.5) | collective-permute-done | bytes 118816 | tf_op jit(solution)/shard_map/ppermute | solution.py:23
  22.6 0.1 pad_maximum_fusion.1.refs_2_
  22.7 0.0 collective-permute-start.6
  22.7 1.1 %collective-permute-done.10 = bf16[16,3584]{1,0:T(8,128)(2,1)S(1)} collective-permute-done((bf16[16,3584]{1,0:T(8,128)(2,1)S(1)}, bf16[16,3584]{1,0:T(8,128)(2,1)S(1)}, u32[]{:S(2)}, u32[]{:S(2)}) %collective-permute-start.10) | collective-permute-done | bytes 114720 | tf_op jit(solution)/shard_map/ppermute | solution.py:23
  23.9 0.0 collective-permute-done.6.refs_3_.refs_1_
  23.9 0.2 collective-permute-start.11
  24.1 0.1 broadcast_in_dim.6
  24.2 0.1 broadcast_in_dim_reshape.3.refs_1_
  24.3 0.0 collective-permute-done.9.refs_5_
  24.3 0.9 %shard_map.72 = (bf16[192,3584]{1,0:T(8,128)(2,1)S(1)}, s32[1,256]{1,0:T(1,128)S(1)}, f32[1,256]{1,0:T(1,128)S(1)}) custom-call(s32[1]{0:T(128)} %bitcast.refs_0_.me_ref, s32[1,256]{1,0:T(1,128)S(1)} %broadcast_in_dim_reshape.3.refs_1_, bf16[16,256]{1,0:T(8,128)(2,1)S(1)} %pad_maximum_fusion.1.refs_2_, ...), custom_call_target="tpu_custom_call" | custom-call | tf_op jit(solution)/shard_map/pallas_call | solution.py:285
  25.2 0.3 collective-permute-done.11.refs_1_
  25.5 5.2 %shard_map.74 = bf16[256,2048]{1,0:T(8,128)(2,1)} custom-call(s32[1]{0:T(128)} %bitcast.refs_0_.me_ref, s32[1,256]{1,0:T(1,128)S(1)} %get-tuple-element.11.slot_ref, f32[1,256]{1,0:T(1,128)S(1)} %get-tuple-element.12.gate_ref, bf16[256,2048]{1,0:T(8,128)(2,1)S(1)} %get-tuple-element.13.saved_ref, bf16[1024,3584]{1,0:T(8,128)(2,1)} %bitcast.11, ...), custom_call_target="tpu_custom_call" | custom-call | tf_op jit(solution)/shard_map/pallas_call | solution.py:303
  (14 shorter events, 0.1 us)
Async XLA Ops:
  0.0 12.4 %collective-permute-start.1 = (bf16[16,3584]{1,0:T(8,128)(2,1)}, bf16[16,3584]{1,0:T(8,128)(2,1)S(1)}, u32[]{:S(2)}, u32[]{:S(2)}) collective-permute-start(bf16[16,3584]{1,0:T(8,128)(2,1)} %bitcast.15), channel_id=1, source_target_pairs={{0,24},{1,25},{2,26},{3,27},{4,28},{5,29},{6,30},{7,31},{8,16},{9,... | collective-permute-start | bytes 344072 | tf_op jit(solution)/shard_map/ppermute | solution.py:33
  5.0 10.0 %collective-permute-start.4 = (bf16[16,3584]{1,0:T(8,128)(2,1)}, bf16[16,3584]{1,0:T(8,128)(2,1)S(1)}, u32[]{:S(2)}, u32[]{:S(2)}) collective-permute-start(bf16[16,3584]{1,0:T(8,128)(2,1)} %bitcast.16), channel_id=1, source_target_pairs={{0,18},{1,19},{2,16},{3,17},{4,22},{5,23},{6,20},{7,21},{8,26},{9,... | collective-permute-start | bytes 344072 | tf_op jit(solution)/shard_map/ppermute | solution.py:33
  7.7 4.6 %collective-permute-start = (bf16[16,32]{1,0:T(8,128)(2,1)S(1)}, bf16[16,32]{1,0:T(8,128)(2,1)S(1)}, u32[]{:S(2)}, u32[]{:S(2)}) collective-permute-start(bf16[16,32]{1,0:T(8,128)(2,1)S(1)} %get-tuple-element.10), channel_id=1, source_target_pairs={{0,8},{1,9},{2,10},{3,11},{4,12},{5,13},{6,14},{7,15},{8,0},{9,1},... | collective-permute-start | bytes 3080 | tf_op jit(solution)/shard_map/ppermute | solution.py:23
  8.1 6.8 %collective-permute-start.3 = (bf16[16,3584]{1,0:T(8,128)(2,1)}, bf16[16,3584]{1,0:T(8,128)(2,1)S(1)}, u32[]{:S(2)}, u32[]{:S(2)}) collective-permute-start(bf16[16,3584]{1,0:T(8,128)(2,1)} %bitcast.17), channel_id=1, source_target_pairs={{0,20},{1,21},{2,22},{3,23},{4,16},{5,17},{6,18},{7,19},{8,28},{9,... | collective-permute-start | bytes 344072 | tf_op jit(solution)/shard_map/ppermute | solution.py:33
  10.7 6.3 %collective-permute-start.7 = (bf16[16,3584]{1,0:T(8,128)(2,1)}, bf16[16,3584]{1,0:T(8,128)(2,1)S(1)}, u32[]{:S(2)}, u32[]{:S(2)}) collective-permute-start(bf16[16,3584]{1,0:T(8,128)(2,1)} %bitcast.18), channel_id=1, source_target_pairs={{0,16},{1,17},{2,18},{3,19},{4,20},{5,21},{6,22},{7,23},{8,24},{9,... | collective-permute-start | bytes 344072 | tf_op jit(solution)/shard_map/ppermute | solution.py:33
  12.4 4.9 %collective-permute-start.2 = (bf16[16,3648]{1,0:T(8,128)(2,1)S(1)}, bf16[16,3648]{1,0:T(8,128)(2,1)S(1)}, u32[]{:S(2)}, u32[]{:S(2)}) collective-permute-start(bf16[16,3648]{1,0:T(8,128)(2,1)S(1)} %shard_map.70), channel_id=1, source_target_pairs={{0,4},{1,5},{2,6},{3,7},{4,0},{5,1},{6,2},{7,3},{8,12},{9,13},{10,... | collective-permute-start | bytes 350216 | tf_op jit(solution)/shard_map/ppermute | solution.py:23
  14.1 5.5 %collective-permute-start.8 = (bf16[16,3584]{1,0:T(8,128)(2,1)S(1)}, bf16[16,3584]{1,0:T(8,128)(2,1)S(1)}, u32[]{:S(2)}, u32[]{:S(2)}) collective-permute-start(bf16[16,3584]{1,0:T(8,128)(2,1)S(1)} %collective-permute-done.1.refs_0_), channel_id=1, source_target_pairs={{0,2},{1,3},{2,0},{3,1},{4,6},{5,7},{6,4},{7,5},{8,10},{9,11},{10,... | collective-permute-start | bytes 344072 | tf_op jit(solution)/shard_map/ppermute | solution.py:23
  17.4 5.2 %collective-permute-start.5 = (bf16[16,3712]{1,0:T(8,128)(2,1)S(1)}, bf16[16,3712]{1,0:T(8,128)(2,1)S(1)}, u32[]{:S(2)}, u32[]{:S(2)}) collective-permute-start(bf16[16,3712]{1,0:T(8,128)(2,1)S(1)} %shard_map.71), channel_id=1, source_target_pairs={{0,2},{1,3},{2,0},{3,1},{4,6},{5,7},{6,4},{7,5},{8,10},{9,11},{10,... | collective-permute-start | bytes 356360 | tf_op jit(solution)/shard_map/ppermute | solution.py:23
  18.0 5.8 %collective-permute-start.10 = (bf16[16,3584]{1,0:T(8,128)(2,1)S(1)}, bf16[16,3584]{1,0:T(8,128)(2,1)S(1)}, u32[]{:S(2)}, u32[]{:S(2)}) collective-permute-start(bf16[16,3584]{1,0:T(8,128)(2,1)S(1)} %get-tuple-element.15), channel_id=1, source_target_pairs={{0,2},{1,3},{2,0},{3,1},{4,6},{5,7},{6,4},{7,5},{8,10},{9,11},{10,... | collective-permute-start | bytes 344072 | tf_op jit(solution)/shard_map/ppermute | solution.py:23
  19.6 4.7 %collective-permute-start.9 = (bf16[96,3584]{1,0:T(8,128)(2,1)S(1)}, bf16[96,3584]{1,0:T(8,128)(2,1)S(1)}, u32[]{:S(2)}, u32[]{:S(2)}) collective-permute-start(bf16[96,3584]{1,0:T(8,128)(2,1)S(1)} %constant_dynamic-update-slice_fusion.refs_4_), channel_id=1, source_target_pairs={{0,1},{1,0},{2,3},{3,2},{4,5},{5,4},{6,7},{7,6},{8,9},{9,8},{10,11... | collective-permute-start | bytes 2064392 | tf_op jit(solution)/shard_map/ppermute | solution.py:23
  22.7 1.2 %collective-permute-start.6 = (bf16[16,256]{1,0:T(8,128)(2,1)S(1)}, bf16[16,256]{1,0:T(8,128)(2,1)S(1)}, u32[]{:S(2)}, u32[]{:S(2)}) collective-permute-start(bf16[16,256]{1,0:T(8,128)(2,1)S(1)} %pad_maximum_fusion.1.refs_2_), channel_id=1, source_target_pairs={{0,1},{1,0},{2,3},{3,2},{4,5},{5,4},{6,7},{7,6},{8,9},{9,8},{10,11... | collective-permute-start | bytes 24584 | tf_op jit(solution)/shard_map/ppermute | solution.py:23
  23.9 1.6 %collective-permute-start.11 = (bf16[32,3584]{1,0:T(8,128)(2,1)S(1)}, bf16[32,3584]{1,0:T(8,128)(2,1)S(1)}, u32[]{:S(2)}, u32[]{:S(2)}) collective-permute-start(bf16[32,3584]{1,0:T(8,128)(2,1)S(1)} %shard_map.73.refs_0_), channel_id=1, source_target_pairs={{0,1},{1,0},{2,3},{3,2},{4,5},{5,4},{6,7},{7,6},{8,9},{9,8},{10,11... | collective-permute-start | bytes 688136 | tf_op jit(solution)/shard_map/ppermute | solution.py:23

commit v5 on v4

--- a/solution.py
+++ b/solution.py
@@ -146,12 +146,15 @@
 
 def slot_bases(order, most, tok, me):
     blocks, units = slot_units(order, most)
-    deltas = jnp.asarray(order, jnp.int32)
-    starts = jnp.asarray([units.index(delta // blocks) * blocks * most for delta in order], jnp.int32)
-    return jnp.repeat(starts + (me ^ deltas) % blocks * most, tok)[None, :]
-
-
-def find_slots(order, table_order, tok, me, base_ref, table_refs, table_ref):
+    part = lax.broadcasted_iota(jnp.int32, (1, len(order) * tok), 1) // tok
+    bases = jnp.zeros_like(part)
+    for i, delta in enumerate(order):
+        base = units.index(delta // blocks) * blocks * most + (me ^ delta) % blocks * most
+        bases = jnp.where(part == i, base, bases)
+    return bases
+
+
+def find_slots(order, table_order, tok, most, me, table_refs, table_ref):
     experts = table_ref.shape[1] // 2
     count = len(order) * tok
     for names, ref in zip(table_order, table_refs, strict=True):
@@ -171,7 +174,7 @@
         (((1,), (0,)), ((), ())),
         preferred_element_type=jnp.float32,
     )
-    slot = jnp.where(live[:1], base_ref[...] + before[:1].astype(jnp.int32), -1)
+    slot = jnp.where(live[:1], slot_bases(order, most, tok, me) + before[:1].astype(jnp.int32), -1)
     return slot, gate[:1]
 
 
@@ -190,11 +193,18 @@
 
 
 def arrange_kernel(order, table_order, tok, most, *refs):
-    me_ref, base_ref = refs[:2]
+    me_ref, w_hbm = refs[:2]
     table_refs = refs[2 : 2 + len(table_order)]
-    token_refs = refs[2 + len(table_order) : -4]
-    rows_ref, slot_ref, gate_ref, table_ref = refs[-4:]
-    slot, gate = find_slots(order, table_order, tok, me_ref[0], base_ref, table_refs, table_ref)
+    token_refs = refs[2 + len(table_order) : -6]
+    rows_ref, slot_ref, gate_ref, w_ref, table_ref, sems = refs[-6:]
+    tall = w_ref.shape[0] // W_LOADS
+    loads = [
+        pltpu.make_async_copy(w_hbm.at[pl.ds(n * tall, tall)], w_ref.at[pl.ds(n * tall, tall)], sems.at[n])
+        for n in range(W_LOADS)
+    ]
+    for load in loads:
+        load.start()
+    slot, gate = find_slots(order, table_order, tok, most, me_ref[0], table_refs, table_ref)
     slot_ref[...] = slot
     gate_ref[...] = gate
     token, row = 0, 0
@@ -202,14 +212,16 @@
         count = ref.shape[0]
         height = count // tok * most
         span = slice(token, token + count)
-        if rows_ref.shape[0] < base_ref.shape[1] // tok * most:
+        if most >= ROWS:
             fill_rows(rows_ref, ref, slot[:, span], gate[:, span], row, height)
         else:
             fill_rows(rows_ref, ref, slot[:, span], gate[:, span], 0, rows_ref.shape[0], add=token > 0)
         token, row = token + count, row + height
-
-
-def down_kernel(order, tok, most, me_ref, slot_ref, gate_ref, saved_ref, w_hbm, early_ref, *refs):
+    for load in loads:
+        load.wait()
+
+
+def down_kernel(order, tok, most, me_ref, slot_ref, gate_ref, saved_ref, first_ref, w_hbm, early_ref, *refs):
     token_refs, (out_hbm, d_ref, w_ref, out_ref, sems, out_sems) = refs[:-6], refs[-6:]
     width = w_ref.shape[0]
     blocks, units = slot_units(order, most)
@@ -227,8 +239,11 @@
             span = pl.ds(pl.multiple_of(half * width + part * wide, wide), wide)
             yield pltpu.make_async_copy(out_ref.at[:, span], out_hbm.at[:, span], out_sems.at[2 * part + half])
 
-    for n in range(W_PARTS * W_LOADS):
+    for n in range(W_LOADS, W_PARTS * W_LOADS):
         load(n).start()
+    for n in range(W_LOADS):
+        part = pl.ds(n * height, height)
+        pltpu.make_async_copy(first_ref.at[part], w_ref.at[part], sems.at[n]).start()
     row = early_ref.shape[0]
     d_ref[:row, :] = early_ref[...]
     token = len(order) * tok - sum(ref.shape[0] for ref in token_refs)
@@ -282,20 +297,24 @@
     vmem, hbm = pl.BlockSpec(memory_space=pltpu.VMEM), pl.BlockSpec(memory_space=pl.ANY)
     count = experts * tok
     early = early_own[1].shape[0] * 2 // tok * most if most >= ROWS else slots
-    rows, slot, gate = pl.pallas_call(
+    rows, slot, gate, first = pl.pallas_call(
         functools.partial(arrange_kernel, order, [names for names, _ in tables], tok, most),
         out_shape=[
             jax.ShapeDtypeStruct((early, features), jnp.bfloat16),
             jax.ShapeDtypeStruct((1, count), jnp.int32),
             jax.ShapeDtypeStruct((1, count), jnp.float32),
-        ],
-        in_specs=[smem] + [vmem] * (1 + len(tables) + 2),
-        out_specs=[vmem] * 3,
-        scratch_shapes=[pltpu.VMEM((count, 2 * experts), jnp.bfloat16)],
+            jax.ShapeDtypeStruct((width // 2 // W_PARTS, features), w_down.dtype),
+        ],
+        in_specs=[smem, hbm] + [vmem] * (len(tables) + 2),
+        out_specs=[vmem] * 4,
+        scratch_shapes=[
+            pltpu.VMEM((count, 2 * experts), jnp.bfloat16),
+            pltpu.SemaphoreType.DMA((W_LOADS,)),
+        ],
         compiler_params=pltpu.CompilerParams(vmem_limit_bytes=16 * MIB),
     )(
         me,
-        slot_bases(order, most, tok, me),
+        in_space(w_down[0], pltpu.HBM),
         *[array for _, array in tables],
         early_own[1],
         early_other[1],
@@ -303,7 +322,7 @@
     out = pl.pallas_call(
         functools.partial(down_kernel, order, tok, most),
         out_shape=jax.ShapeDtypeStruct((slots, width), jnp.bfloat16),
-        in_specs=[smem, vmem, vmem, vmem, hbm, vmem, vmem, vmem],
+        in_specs=[smem, vmem, vmem, vmem, vmem, hbm, vmem, vmem, vmem],
         out_specs=hbm,
         scratch_shapes=[
             pltpu.VMEM((slots, features), jnp.bfloat16),
@@ -318,6 +337,7 @@
         slot,
         gate,
         near_saved,
+        first,
         in_space(w_down[0], pltpu.HBM),
         rows,
         late_own[1],

time: 30.9 us -> 30.7 us (level)
  Pallas kernels: 7.42 us -> 7.73 us
    pallas_call x1, Pallas kernels: 0.86 us -> 1.97 us  [per_device(): pl.pallas_call(functools.partial(arrange_kernel, order, [names for names,...]
    pallas_call x1, Pallas kernels: 5.24 us -> 4.44 us  [per_device(): pl.pallas_call(functools.partial(down_kernel, order, tok, most), out_shap...]
  transfers between devices with their start and end apart: 12 -> 12, of which waited for: 7 -> 6; matrix products, arithmetic and copies ran while one was open for 2% -> 1% of each run, Pallas kernels for 7% -> 11%
where the time goes in v5:
time: 30.7 us; the launch traced here: 30.6 us
  starting transfers between devices  14.5 us (47%)
  waiting for transfers between devices  7.88 us (26%)
  Pallas kernels  7.73 us (25%)
    ppermute x4, starting transfers between devices, from_next_section(): return lax.ppermute(x, ('section', 'expert'), pairs)  9.49 us
    ppermute x8, waiting for transfers between devices, exchange(): return lax.ppermute(x, 'expert', [(i, i ^ delta) for i in range(peers)])  5.53 us
    ppermute x8, starting transfers between devices, exchange(): return lax.ppermute(x, 'expert', [(i, i ^ delta) for i in range(peers)])  5.01 us
    pallas_call x1, Pallas kernels, per_device(): pl.pallas_call(functools.partial(down_kernel, order, tok, most), out_shap...  4.44 us
    ppermute x4, waiting for transfers between devices, from_next_section(): return lax.ppermute(x, ('section', 'expert'), pairs)  2.35 us
    pallas_call x1, Pallas kernels, per_device(): pl.pallas_call(functools.partial(arrange_kernel, order, [names for names,...  1.97 us
    pallas_call x1, Pallas kernels, assign_table(): pl.pallas_call(table_kernel, out_shape=[jax.ShapeDtypeStruct((routes.shap...  1.28 us
  transfers between devices with their start and end apart: 12, of which 6 were waited for; matrix products, arithmetic and copies ran while one was open for 1% of the time, Pallas kernels for 11%

profile of v5, /device:TPU:0, one launch (start us, length us, event | category | flops | bytes accessed | tf_op | source)
XLA Modules:
  0.0 30.6 jit_solution(14502188429381831627)
XLA Ops:
  0.0 5.0 %collective-permute-start.1 = (bf16[16,3584]{1,0:T(8,128)(2,1)}, bf16[16,3584]{1,0:T(8,128)(2,1)S(1)}, u32[]{:S(2)}, u32[]{:S(2)}) collective-permute-start(bf16[16,3584]{1,0:T(8,128)(2,1)} %bitcast.16), channel_id=1, source_target_pairs={{0,24},{1,25},{2,26},{3,27},{4,28},{5,29},{6,30},{7,31},{8,16},{9,... | collective-permute-start | bytes 344072 | tf_op jit(solution)/shard_map/ppermute | solution.py:33
  5.0 1.5 %collective-permute-start.4 = (bf16[16,3584]{1,0:T(8,128)(2,1)}, bf16[16,3584]{1,0:T(8,128)(2,1)S(1)}, u32[]{:S(2)}, u32[]{:S(2)}) collective-permute-start(bf16[16,3584]{1,0:T(8,128)(2,1)} %bitcast.17), channel_id=1, source_target_pairs={{0,18},{1,19},{2,16},{3,17},{4,22},{5,23},{6,20},{7,21},{8,26},{9,... | collective-permute-start | bytes 344072 | tf_op jit(solution)/shard_map/ppermute | solution.py:33
  6.5 1.3 %shard_map.55 = (bf16[16,32]{1,0:T(8,128)(2,1)S(1)}, bf16[256,2048]{1,0:T(8,128)(2,1)S(1)}) custom-call(s32[8,16]{1,0:T(8,128)} %bitcast.14, f32[8,16]{1,0:T(8,128)} %bitcast.15, bf16[256,2048]{1,0:T(8,128)(2,1)} %bitcast.13), custom_call_target="tpu_custom_call" | custom-call | tf_op jit(solution)/shard_map/pallas_call | solution.py:60
  7.7 0.4 %collective-permute-start = (bf16[16,32]{1,0:T(8,128)(2,1)S(1)}, bf16[16,32]{1,0:T(8,128)(2,1)S(1)}, u32[]{:S(2)}, u32[]{:S(2)}) collective-permute-start(bf16[16,32]{1,0:T(8,128)(2,1)S(1)} %get-tuple-element.11), channel_id=1, source_target_pairs={{0,8},{1,9},{2,10},{3,11},{4,12},{5,13},{6,14},{7,15},{8,0},{9,1},... | collective-permute-start | bytes 3080 | tf_op jit(solution)/shard_map/ppermute | solution.py:23
  8.1 2.5 %collective-permute-start.3 = (bf16[16,3584]{1,0:T(8,128)(2,1)}, bf16[16,3584]{1,0:T(8,128)(2,1)S(1)}, u32[]{:S(2)}, u32[]{:S(2)}) collective-permute-start(bf16[16,3584]{1,0:T(8,128)(2,1)} %bitcast.18), channel_id=1, source_target_pairs={{0,20},{1,21},{2,22},{3,23},{4,16},{5,17},{6,18},{7,19},{8,28},{9,... | collective-permute-start | bytes 344072 | tf_op jit(solution)/shard_map/ppermute | solution.py:33
  10.7 0.5 %collective-permute-start.7 = (bf16[16,3584]{1,0:T(8,128)(2,1)}, bf16[16,3584]{1,0:T(8,128)(2,1)S(1)}, u32[]{:S(2)}, u32[]{:S(2)}) collective-permute-start(bf16[16,3584]{1,0:T(8,128)(2,1)} %bitcast.19), channel_id=1, source_target_pairs={{0,16},{1,17},{2,18},{3,19},{4,20},{5,21},{6,22},{7,23},{8,24},{9,... | collective-permute-start | bytes 344072 | tf_op jit(solution)/shard_map/ppermute | solution.py:33
  11.2 1.1 %collective-permute-done = bf16[16,32]{1,0:T(8,128)(2,1)S(1)} collective-permute-done((bf16[16,32]{1,0:T(8,128)(2,1)S(1)}, bf16[16,32]{1,0:T(8,128)(2,1)S(1)}, u32[]{:S(2)}, u32[]{:S(2)}) %collective-permute-start) | collective-permute-done | bytes 1056 | tf_op jit(solution)/shard_map/ppermute | solution.py:23
  12.3 0.1 pad_maximum_fusion.2.refs_1_
  12.4 0.0 collective-permute-done.1.refs_0_
  12.4 1.6 %collective-permute-start.2 = (bf16[16,3648]{1,0:T(8,128)(2,1)S(1)}, bf16[16,3648]{1,0:T(8,128)(2,1)S(1)}, u32[]{:S(2)}, u32[]{:S(2)}) collective-permute-start(bf16[16,3648]{1,0:T(8,128)(2,1)S(1)} %shard_map.56), channel_id=1, source_target_pairs={{0,4},{1,5},{2,6},{3,7},{4,0},{5,1},{6,2},{7,3},{8,12},{9,13},{10,... | collective-permute-start | bytes 350216 | tf_op jit(solution)/shard_map/ppermute | solution.py:23
  14.1 0.5 %collective-permute-start.8 = (bf16[16,3584]{1,0:T(8,128)(2,1)S(1)}, bf16[16,3584]{1,0:T(8,128)(2,1)S(1)}, u32[]{:S(2)}, u32[]{:S(2)}) collective-permute-start(bf16[16,3584]{1,0:T(8,128)(2,1)S(1)} %collective-permute-done.1.refs_0_), channel_id=1, source_target_pairs={{0,2},{1,3},{2,0},{3,1},{4,6},{5,7},{6,4},{7,5},{8,10},{9,11},{10,... | collective-permute-start | bytes 344072 | tf_op jit(solution)/shard_map/ppermute | solution.py:23
  14.6 0.4 %collective-permute-done.4.refs_2_ = bf16[16,3584]{1,0:T(8,128)(2,1)S(1)} collective-permute-done((bf16[16,3584]{1,0:T(8,128)(2,1)}, bf16[16,3584]{1,0:T(8,128)(2,1)S(1)}, u32[]{:S(2)}, u32[]{:S(2)}) %collective-permute-start.4) | collective-permute-done | bytes 114720 | tf_op jit(solution)/shard_map/ppermute | solution.py:33
  15.0 0.0 collective-permute-done.3.refs_0_
  15.0 2.0 %collective-permute-done.7 = bf16[16,3584]{1,0:T(8,128)(2,1)S(1)} collective-permute-done((bf16[16,3584]{1,0:T(8,128)(2,1)}, bf16[16,3584]{1,0:T(8,128)(2,1)S(1)}, u32[]{:S(2)}, u32[]{:S(2)}) %collective-permute-start.7) | collective-permute-done | bytes 114720 | tf_op jit(solution)/shard_map/ppermute | solution.py:33
  17.0 0.3 %collective-permute-done.2 = bf16[16,3648]{1,0:T(8,128)(2,1)S(1)} collective-permute-done((bf16[16,3648]{1,0:T(8,128)(2,1)S(1)}, bf16[16,3648]{1,0:T(8,128)(2,1)S(1)}, u32[]{:S(2)}, u32[]{:S(2)}) %collective-permute-start.2) | collective-permute-done | bytes 116768 | tf_op jit(solution)/shard_map/ppermute | solution.py:23
  17.3 0.1 pad_maximum_fusion.3.refs_1_
  17.4 0.6 %collective-permute-start.5 = (bf16[16,3712]{1,0:T(8,128)(2,1)S(1)}, bf16[16,3712]{1,0:T(8,128)(2,1)S(1)}, u32[]{:S(2)}, u32[]{:S(2)}) collective-permute-start(bf16[16,3712]{1,0:T(8,128)(2,1)S(1)} %shard_map.57), channel_id=1, source_target_pairs={{0,2},{1,3},{2,0},{3,1},{4,6},{5,7},{6,4},{7,5},{8,10},{9,11},{10,... | collective-permute-start | bytes 356360 | tf_op jit(solution)/shard_map/ppermute | solution.py:23
  18.0 1.6 %collective-permute-start.10 = (bf16[16,3584]{1,0:T(8,128)(2,1)S(1)}, bf16[16,3584]{1,0:T(8,128)(2,1)S(1)}, u32[]{:S(2)}, u32[]{:S(2)}) collective-permute-start(bf16[16,3584]{1,0:T(8,128)(2,1)S(1)} %get-tuple-element.17), channel_id=1, source_target_pairs={{0,2},{1,3},{2,0},{3,1},{4,6},{5,7},{6,4},{7,5},{8,10},{9,11},{10,... | collective-permute-start | bytes 344072 | tf_op jit(solution)/shard_map/ppermute | solution.py:23
  19.6 0.0 collective-permute-done.8
  19.6 0.1 collective-permute-start.9
  19.7 2.9 %collective-permute-done.5 = bf16[16,3712]{1,0:T(8,128)(2,1)S(1)} collective-permute-done((bf16[16,3712]{1,0:T(8,128)(2,1)S(1)}, bf16[16,3712]{1,0:T(8,128)(2,1)S(1)}, u32[]{:S(2)}, u32[]{:S(2)}) %collective-permute-start.5) | collective-permute-done | bytes 118816 | tf_op jit(solution)/shard_map/ppermute | solution.py:23
  22.6 0.1 pad_maximum_fusion.1.refs_2_
  22.7 0.0 collective-permute-start.6
  22.7 1.1 %collective-permute-done.10 = bf16[16,3584]{1,0:T(8,128)(2,1)S(1)} collective-permute-done((bf16[16,3584]{1,0:T(8,128)(2,1)S(1)}, bf16[16,3584]{1,0:T(8,128)(2,1)S(1)}, u32[]{:S(2)}, u32[]{:S(2)}) %collective-permute-start.10) | collective-permute-done | bytes 114720 | tf_op jit(solution)/shard_map/ppermute | solution.py:23
  23.9 0.0 collective-permute-done.6.refs_3_.refs_1_
  23.9 0.2 collective-permute-start.11
  24.1 0.0 collective-permute-done.9.refs_5_
  24.1 2.0 %shard_map.58 = (bf16[192,3584]{1,0:T(8,128)(2,1)S(1)}, s32[1,256]{1,0:T(1,128)S(1)}, f32[1,256]{1,0:T(1,128)S(1)}, bf16[256,3584]{1,0:T(8,128)(2,1)S(1)}) custom-call(s32[1]{0:T(128)} %bitcast.refs_0_.me_ref, bf16[1024,3584]{1,0:T(8,128)(2,1)} %bitcast.11, bf16[16,256]{1,0:T(8,128)(2,1)S(1)} %pad_maximum_fusion.1.refs_2_, ...), custom_call_target="tpu_custom_call" | custom-call | tf_op jit(solution)/shard_map/pallas_call | solution.py:300
  26.1 0.0 collective-permute-done.11.refs_1_
  26.1 4.4 %shard_map.60 = bf16[256,2048]{1,0:T(8,128)(2,1)} custom-call(s32[1]{0:T(128)} %bitcast.refs_0_.me_ref, s32[1,256]{1,0:T(1,128)S(1)} %get-tuple-element.12.slot_ref, f32[1,256]{1,0:T(1,128)S(1)} %get-tuple-element.13.gate_ref, bf16[256,2048]{1,0:T(8,128)(2,1)S(1)} %get-tuple-element.14.saved_ref, bf16[256,3584]{1,0:T(8,128)(2,1)S(1)} %get-tuple-element.15.first_ref, ...), custom_call_target="tpu_custom_call" | custom-call | tf_op jit(solution)/shard_map/pallas_call | solution.py:322
  (13 shorter events, 0.1 us)
Async XLA Ops:
  0.0 12.4 %collective-permute-start.1 = (bf16[16,3584]{1,0:T(8,128)(2,1)}, bf16[16,3584]{1,0:T(8,128)(2,1)S(1)}, u32[]{:S(2)}, u32[]{:S(2)}) collective-permute-start(bf16[16,3584]{1,0:T(8,128)(2,1)} %bitcast.16), channel_id=1, source_target_pairs={{0,24},{1,25},{2,26},{3,27},{4,28},{5,29},{6,30},{7,31},{8,16},{9,... | collective-permute-start | bytes 344072 | tf_op jit(solution)/shard_map/ppermute | solution.py:33
  5.0 10.0 %collective-permute-start.4 = (bf16[16,3584]{1,0:T(8,128)(2,1)}, bf16[16,3584]{1,0:T(8,128)(2,1)S(1)}, u32[]{:S(2)}, u32[]{:S(2)}) collective-permute-start(bf16[16,3584]{1,0:T(8,128)(2,1)} %bitcast.17), channel_id=1, source_target_pairs={{0,18},{1,19},{2,16},{3,17},{4,22},{5,23},{6,20},{7,21},{8,26},{9,... | collective-permute-start | bytes 344072 | tf_op jit(solution)/shard_map/ppermute | solution.py:33
  7.7 4.6 %collective-permute-start = (bf16[16,32]{1,0:T(8,128)(2,1)S(1)}, bf16[16,32]{1,0:T(8,128)(2,1)S(1)}, u32[]{:S(2)}, u32[]{:S(2)}) collective-permute-start(bf16[16,32]{1,0:T(8,128)(2,1)S(1)} %get-tuple-element.11), channel_id=1, source_target_pairs={{0,8},{1,9},{2,10},{3,11},{4,12},{5,13},{6,14},{7,15},{8,0},{9,1},... | collective-permute-start | bytes 3080 | tf_op jit(solution)/shard_map/ppermute | solution.py:23
  8.1 6.8 %collective-permute-start.3 = (bf16[16,3584]{1,0:T(8,128)(2,1)}, bf16[16,3584]{1,0:T(8,128)(2,1)S(1)}, u32[]{:S(2)}, u32[]{:S(2)}) collective-permute-start(bf16[16,3584]{1,0:T(8,128)(2,1)} %bitcast.18), channel_id=1, source_target_pairs={{0,20},{1,21},{2,22},{3,23},{4,16},{5,17},{6,18},{7,19},{8,28},{9,... | collective-permute-start | bytes 344072 | tf_op jit(solution)/shard_map/ppermute | solution.py:33
  10.7 6.3 %collective-permute-start.7 = (bf16[16,3584]{1,0:T(8,128)(2,1)}, bf16[16,3584]{1,0:T(8,128)(2,1)S(1)}, u32[]{:S(2)}, u32[]{:S(2)}) collective-permute-start(bf16[16,3584]{1,0:T(8,128)(2,1)} %bitcast.19), channel_id=1, source_target_pairs={{0,16},{1,17},{2,18},{3,19},{4,20},{5,21},{6,22},{7,23},{8,24},{9,... | collective-permute-start | bytes 344072 | tf_op jit(solution)/shard_map/ppermute | solution.py:33
  12.4 4.9 %collective-permute-start.2 = (bf16[16,3648]{1,0:T(8,128)(2,1)S(1)}, bf16[16,3648]{1,0:T(8,128)(2,1)S(1)}, u32[]{:S(2)}, u32[]{:S(2)}) collective-permute-start(bf16[16,3648]{1,0:T(8,128)(2,1)S(1)} %shard_map.56), channel_id=1, source_target_pairs={{0,4},{1,5},{2,6},{3,7},{4,0},{5,1},{6,2},{7,3},{8,12},{9,13},{10,... | collective-permute-start | bytes 350216 | tf_op jit(solution)/shard_map/ppermute | solution.py:23
  14.1 5.5 %collective-permute-start.8 = (bf16[16,3584]{1,0:T(8,128)(2,1)S(1)}, bf16[16,3584]{1,0:T(8,128)(2,1)S(1)}, u32[]{:S(2)}, u32[]{:S(2)}) collective-permute-start(bf16[16,3584]{1,0:T(8,128)(2,1)S(1)} %collective-permute-done.1.refs_0_), channel_id=1, source_target_pairs={{0,2},{1,3},{2,0},{3,1},{4,6},{5,7},{6,4},{7,5},{8,10},{9,11},{10,... | collective-permute-start | bytes 344072 | tf_op jit(solution)/shard_map/ppermute | solution.py:23
  17.4 5.2 %collective-permute-start.5 = (bf16[16,3712]{1,0:T(8,128)(2,1)S(1)}, bf16[16,3712]{1,0:T(8,128)(2,1)S(1)}, u32[]{:S(2)}, u32[]{:S(2)}) collective-permute-start(bf16[16,3712]{1,0:T(8,128)(2,1)S(1)} %shard_map.57), channel_id=1, source_target_pairs={{0,2},{1,3},{2,0},{3,1},{4,6},{5,7},{6,4},{7,5},{8,10},{9,11},{10,... | collective-permute-start | bytes 356360 | tf_op jit(solution)/shard_map/ppermute | solution.py:23
  18.0 5.8 %collective-permute-start.10 = (bf16[16,3584]{1,0:T(8,128)(2,1)S(1)}, bf16[16,3584]{1,0:T(8,128)(2,1)S(1)}, u32[]{:S(2)}, u32[]{:S(2)}) collective-permute-start(bf16[16,3584]{1,0:T(8,128)(2,1)S(1)} %get-tuple-element.17), channel_id=1, source_target_pairs={{0,2},{1,3},{2,0},{3,1},{4,6},{5,7},{6,4},{7,5},{8,10},{9,11},{10,... | collective-permute-start | bytes 344072 | tf_op jit(solution)/shard_map/ppermute | solution.py:23
  19.6 4.5 %collective-permute-start.9 = (bf16[96,3584]{1,0:T(8,128)(2,1)S(1)}, bf16[96,3584]{1,0:T(8,128)(2,1)S(1)}, u32[]{:S(2)}, u32[]{:S(2)}) collective-permute-start(bf16[96,3584]{1,0:T(8,128)(2,1)S(1)} %constant_dynamic-update-slice_fusion.refs_4_), channel_id=1, source_target_pairs={{0,1},{1,0},{2,3},{3,2},{4,5},{5,4},{6,7},{7,6},{8,9},{9,8},{10,11... | collective-permute-start | bytes 2064392 | tf_op jit(solution)/shard_map/ppermute | solution.py:23
  22.7 1.2 %collective-permute-start.6 = (bf16[16,256]{1,0:T(8,128)(2,1)S(1)}, bf16[16,256]{1,0:T(8,128)(2,1)S(1)}, u32[]{:S(2)}, u32[]{:S(2)}) collective-permute-start(bf16[16,256]{1,0:T(8,128)(2,1)S(1)} %pad_maximum_fusion.1.refs_2_), channel_id=1, source_target_pairs={{0,1},{1,0},{2,3},{3,2},{4,5},{5,4},{6,7},{7,6},{8,9},{9,8},{10,11... | collective-permute-start | bytes 24584 | tf_op jit(solution)/shard_map/ppermute | solution.py:23
  23.9 2.2 %collective-permute-start.11 = (bf16[32,3584]{1,0:T(8,128)(2,1)S(1)}, bf16[32,3584]{1,0:T(8,128)(2,1)S(1)}, u32[]{:S(2)}, u32[]{:S(2)}) collective-permute-start(bf16[32,3584]{1,0:T(8,128)(2,1)S(1)} %shard_map.59.refs_0_), channel_id=1, source_target_pairs={{0,1},{1,0},{2,3},{3,2},{4,5},{5,4},{6,7},{7,6},{8,9},{9,8},{10,11... | collective-permute-start | bytes 688136 | tf_op jit(solution)/shard_map/ppermute | solution.py:23
